TPU v7x, 32 devices: a whole 2x2x4 slice. The times are simulated.
32 devices in a mesh: section: 2 (over core), dp: 4 (over z), rep: 4 (over y, x).
Axes of the slice: x: 2, y: 2, z: 4, core: 2. Of those that a mesh axis runs over, the one named last changes fastest.
Arguments:
- inputs: bfloat16 [32768, 512], P(('dp', 'rep')), may hold values from -6 to 6
- cotangent: bfloat16 [32768, 512], P(('dp', 'rep')), may hold values from -6 to 6
- domain_ids: int32 [32], P(('dp', 'rep')), may hold values from 0 to 15
- group_of: int32 [16], replicated, may hold values from 0 to 3
- group_weights: float32 [4], replicated, may hold values from 0.25 to 4
- norm_gains: bfloat16 [2, 2, 512], P('section'), may hold values from 0.5 to 1.5
- norm_biases: bfloat16 [2, 2, 512], P('section'), may hold values from -1.1953125 to 1.1953125
- w_in: bfloat16 [2, 512, 2048], P('section'), may hold values from -0.25 to 0.25
- w_out: bfloat16 [2, 512, 512], P('section'), may hold values from -1 to 1
- w_up: bfloat16 [2, 512, 2048], P('section'), may hold values from -0.25 to 0.25
- in_bias: bfloat16 [2, 2048], P('section'), may hold values from -1.1953125 to 1.1953125
- w_down: bfloat16 [2, 2048, 512], P('section'), may hold values from -0.125 to 0.125
- out_bias: bfloat16 [2, 512], P('section'), may hold values from -1.1953125 to 1.1953125
Outputs:
- layer_outputs: float32 [2, 32768, 512], P('section', ('dp', 'rep'))
- input_grads: float32 [2, 32768, 512], P('section', ('dp', 'rep'))
- g_norm_gains: float32 [2, 2, 512], P('section')
- g_norm_biases: float32 [2, 2, 512], P('section')
- g_w_in: float32 [2, 512, 2048], P('section')
- g_w_out: float32 [2, 512, 512], P('section')
- g_w_up: float32 [2, 512, 2048], P('section')
- g_in_bias: float32 [2, 2048], P('section')
- g_w_down: float32 [2, 2048, 512], P('section')
- g_out_bias: float32 [2, 512], P('section')
- slot_mass: float32 [64], replicated
All inputs are finite; a program needn't handle non-finite values.
Results may differ from a plain program's by a relative error of at most 0.013.
The roundings to bfloat16 on the way count: a program that leaves them out, or rounds other values in their place, can miss the bound.
Values may be sent and summed in bfloat16 or wider, within the bound.
No kernel may reach another device: no remote copies, remote signals or barrier semaphores. Data moves between devices by JAX's collectives and lax.ppermute only.
A program may use at most 576 MiB of HBM per device.

v0:
```python
import jax
import jax.numpy as jnp
from jax import lax
from jax.sharding import PartitionSpec as P

HEADS = 8
DH = 64
SLOTS = 64
BLOCK = 512
MB = 2
LEN = 1024


EPSILON = 1e-05
running_peak_logit = lax.Precision.HIGHEST


def shifted(value, axis, by):
    peers = lax.axis_size(axis)
    pairs = [(i, i + by) for i in range(peers) if 0 <= i + by < peers]
    return lax.ppermute(value, axis, pairs)


def normalize(hidden, gain_row, bias_row):
    center = hidden - jnp.mean(hidden, axis=-1, keepdims=True)
    spread = jnp.mean(center * center, axis=-1, keepdims=True)
    return center * lax.rsqrt(spread + EPSILON) * gain_row + bias_row


def smooth_gate(values):
    return jax.nn.gelu(values, approximate=True)


def multiply(left_low, right_low):
    return jnp.dot(left_low, right_low, preferred_element_type=jnp.float32)


def left_grad(grad_low, right_low):
    return lax.dot_general(
        grad_low, right_low, (((1,), (1,)), ((), ())), preferred_element_type=jnp.float32
    )


def right_grad(left_low, grad_low):
    return lax.dot_general(
        left_low, grad_low, (((0,), (0,)), ((), ())), preferred_element_type=jnp.float32
    )


def slot_block(state_in, segment):
    slot_key_state, slot_value_state, mass_state = state_in
    query_matrix, key_matrix, value_matrix, logits = segment
    softmax_probabilities = jnp.exp(logits)
    extent = softmax_probabilities.shape[1]
    lower = jnp.arange(extent)[:, None] >= jnp.arange(extent)[None, :]
    causal = lower.astype(jnp.float32)
    running_totals = (
        jnp.einsum("ti,him->htm", causal, softmax_probabilities, precision=running_peak_logit)
        + mass_state[:, None, :]
    )
    affinity = jnp.where(
        lower[None],
        jnp.einsum("htd,hid->hti", query_matrix, key_matrix, precision=running_peak_logit),
        0.0,
    )
    score_matrix = jnp.einsum(
        "hti,him->htm", affinity, softmax_probabilities, precision=running_peak_logit
    )
    score_matrix = (
        score_matrix
        + jnp.einsum("byo,bio->byi", query_matrix, slot_key_state, precision=running_peak_logit)
    ) / running_totals
    raised = jnp.exp(score_matrix - jnp.max(score_matrix, axis=-1, keepdims=True))
    chances = raised / jnp.sum(raised, axis=-1, keepdims=True)
    token_segment_part = chances / running_totals
    spread_back = jnp.where(
        lower[None],
        jnp.einsum(
            "htm,him->hti", token_segment_part, softmax_probabilities, precision=running_peak_logit
        ),
        0.0,
    )
    attended_output = jnp.einsum(
        "hti,hid->htd", spread_back, value_matrix, precision=running_peak_logit
    )
    attended_output = attended_output + jnp.einsum(
        "biy,byr->bir", token_segment_part, slot_value_state, precision=running_peak_logit
    )
    slot_key_state = slot_key_state + jnp.einsum(
        "kue,kub->keb", softmax_probabilities, key_matrix, precision=running_peak_logit
    )
    slot_value_state = slot_value_state + jnp.einsum(
        "kue,kub->keb", softmax_probabilities, value_matrix, precision=running_peak_logit
    )
    return (
        (slot_key_state, slot_value_state, running_totals[:, -1, :]),
        (attended_output, jnp.sum(chances, axis=(0, 1))),
    )


def attend(projected):
    length_all = projected.shape[0]
    head_span = HEADS * DH
    blocks = length_all // BLOCK

    def to_blocks(columns, depth):
        return columns.reshape(blocks, BLOCK, HEADS, depth).transpose(0, 2, 1, 3)

    segment = (
        to_blocks(projected[:, :head_span], DH),
        to_blocks(projected[:, head_span : 2 * head_span], DH),
        to_blocks(projected[:, 2 * head_span : 3 * head_span], DH),
        to_blocks(projected[:, 3 * head_span :], SLOTS),
    )
    initial = (
        jnp.zeros((HEADS, SLOTS, DH), jnp.float32),
        jnp.zeros((HEADS, SLOTS, DH), jnp.float32),
        jnp.zeros((HEADS, SLOTS), jnp.float32),
    )
    ending, (outputs, masses) = lax.scan(slot_block, initial, segment)
    return (outputs.transpose(0, 2, 1, 3).reshape(length_all, head_span), jnp.sum(masses, axis=0))


def layer_forward(hidden, parameters):
    gains, biases, w_in, w_out, w_up, in_bias, w_down, out_bias = parameters
    normed = normalize(hidden, gains[0], biases[0]).astype(jnp.bfloat16)
    projected = multiply(normed, w_in)
    attended, masses = attend(projected)
    readout = attended.astype(jnp.bfloat16)
    middle = hidden + multiply(readout, w_out)
    normed_ffn = normalize(middle, gains[1], biases[1]).astype(jnp.bfloat16)
    inner_act = multiply(normed_ffn, w_up) + in_bias
    active = smooth_gate(inner_act).astype(jnp.bfloat16)
    return (middle + multiply(active, w_down) + out_bias, masses)


def layer_backward(hidden, parameters, grad_out):
    gains, biases, w_in, w_out, w_up, in_bias, w_down, out_bias = parameters
    normed_full, pull_first = jax.vjp(normalize, hidden, gains[0], biases[0])
    normed = normed_full.astype(jnp.bfloat16)
    projected = multiply(normed, w_in)
    (attended, masses), pull_attend = jax.vjp(attend, projected)
    readout = attended.astype(jnp.bfloat16)
    middle = hidden + multiply(readout, w_out)
    normed_second, pull_second = jax.vjp(normalize, middle, gains[1], biases[1])
    normed_ffn = normed_second.astype(jnp.bfloat16)
    inner_act = multiply(normed_ffn, w_up) + in_bias
    active_full, pull_gate = jax.vjp(smooth_gate, inner_act)
    active = active_full.astype(jnp.bfloat16)
    grad_low = grad_out.astype(jnp.bfloat16)
    g_out_bias = jnp.sum(grad_out, axis=0)
    g_w_down = right_grad(active, grad_low)
    grad_active = left_grad(grad_low, w_down)
    (grad_inner,) = pull_gate(grad_active)
    g_in_bias = jnp.sum(grad_inner, axis=0)
    inner_low = grad_inner.astype(jnp.bfloat16)
    g_w_up = right_grad(normed_ffn, inner_low)
    grad_second = left_grad(inner_low, w_up)
    grad_mid_norm, g_gain_second, g_bias_second = pull_second(grad_second)
    grad_middle = grad_out + grad_mid_norm
    middle_low = grad_middle.astype(jnp.bfloat16)
    g_w_out = right_grad(readout, middle_low)
    grad_readout = left_grad(middle_low, w_out)
    (grad_projected,) = pull_attend((grad_readout, jnp.zeros_like(masses)))
    projected_low = grad_projected.astype(jnp.bfloat16)
    g_w_in = right_grad(normed, projected_low)
    grad_first = left_grad(projected_low, w_in)
    grad_hid_norm, g_gain_first, g_bias_first = pull_first(grad_first)
    grad_hidden = grad_middle + grad_hid_norm
    grads = (
        jnp.stack([g_gain_first, g_gain_second]),
        jnp.stack([g_bias_first, g_bias_second]),
        g_w_in,
        g_w_out,
        g_w_up,
        g_in_bias,
        g_w_down,
        g_out_bias,
    )
    return (grad_hidden, grads)


def flatten(gradients):
    return jnp.concatenate([piece_grad.reshape(-1) for piece_grad in gradients])


def per_device(
    inputs,
    cotangent,
    domain_ids,
    group_of,
    group_weights,
    norm_gains,
    norm_biases,
    w_in,
    w_out,
    w_up,
    in_bias,
    w_down,
    out_bias,
):
    section = lax.axis_index("section")
    leading = section == 0
    parameters = (
        norm_gains[0].astype(jnp.float32),
        norm_biases[0].astype(jnp.float32),
        w_in[0],
        w_out[0],
        w_up[0],
        in_bias[0].astype(jnp.float32),
        w_down[0],
        out_bias[0].astype(jnp.float32),
    )
    features = inputs.shape[1]
    pieces = inputs.reshape(MB, LEN, features).astype(jnp.float32)
    domain_hits = domain_ids[:, None] == jnp.arange(group_of.shape[0])[None, :]
    groups = jnp.sum(jnp.where(domain_hits, group_of[None, :], 0), axis=1)
    group_hits = groups[:, None] == jnp.arange(group_weights.shape[0])[None, :]
    weights_seq = jnp.sum(jnp.where(group_hits, group_weights[None, :], 0.0), axis=1)
    targets = cotangent.reshape(MB, LEN, features).astype(jnp.float32) * weights_seq[:, None, None]
    blank = jnp.zeros((LEN, features), jnp.float32)
    stored = [blank] * MB
    results = [blank] * MB
    arriving = blank
    slot_total = jnp.zeros((SLOTS,), jnp.float32)
    for moment in range(MB + 1):
        source = jnp.where(leading, pieces[min(moment, MB - 1)], arriving)
        result, masses = layer_forward(source, parameters)
        useful = jnp.where(leading, moment < MB, moment >= 1)
        slot_total = slot_total + jnp.where(useful, masses, 0.0)
        if moment < MB:
            stored[moment] = jnp.where(leading, source, stored[moment])
            results[moment] = jnp.where(leading, result, results[moment])
        if moment >= 1:
            stored[moment - 1] = jnp.where(leading, stored[moment - 1], source)
            results[moment - 1] = jnp.where(leading, results[moment - 1], result)
        if moment < MB:
            arriving = shifted(result.astype(jnp.bfloat16), "section", 1).astype(jnp.float32)
    slot_mass = lax.psum(slot_total / (HEADS * MB * LEN), ("section", "dp", "rep"))
    sizes_all = [weight_arg.size for weight_arg in parameters]
    summed = jnp.zeros((sum(sizes_all),), jnp.float32)
    returning = blank
    grads_in = [blank] * MB
    for moment in range(MB + 1):
        index_high = max(MB - 1 - moment, 0)
        index_low = min(MB - moment, MB - 1)
        source = jnp.where(leading, stored[index_low], stored[index_high])
        own_target = targets[index_high] * (1.0 if moment < MB else 0.0)
        target = jnp.where(leading, returning, own_target)
        grad_source, grad_params = layer_backward(source, parameters, target)
        flattened = flatten(grad_params)
        summed = summed + flattened
        outgoing = grad_source.astype(jnp.bfloat16)
        if moment < MB:
            grads_in[index_high] = jnp.where(
                leading, grads_in[index_high], outgoing.astype(jnp.float32)
            )
        if moment >= 1:
            grads_in[index_low] = jnp.where(leading, grad_source, grads_in[index_low])
        if moment < MB:
            returning = shifted(outgoing, "section", -1).astype(jnp.float32)
    summed = lax.psum(summed, ("dp", "rep"))
    grads_out = []
    offset = 0
    for weight_arg in parameters:
        extent = weight_arg.size
        grads_out.append(summed[offset : offset + extent].reshape(weight_arg.shape)[None])
        offset = offset + extent
    layer_outputs = jnp.concatenate(results, axis=0)[None]
    input_grads = jnp.concatenate(grads_in, axis=0)[None]
    return (
        layer_outputs,
        input_grads,
        grads_out[0],
        grads_out[1],
        grads_out[2],
        grads_out[3],
        grads_out[4],
        grads_out[5],
        grads_out[6],
        grads_out[7],
        slot_mass,
    )


def solution(mesh):
    return jax.shard_map(
        per_device,
        mesh=mesh,
        in_specs=(
            P(("dp", "rep"), None),
            P(("dp", "rep"), None),
            P(("dp", "rep")),
            P(),
            P(),
            P("section", None, None),
            P("section", None, None),
            P("section", None, None),
            P("section", None, None),
            P("section", None, None),
            P("section", None),
            P("section", None, None),
            P("section", None),
        ),
        out_specs=(
            P("section", ("dp", "rep"), None),
            P("section", ("dp", "rep"), None),
            P("section", None, None),
            P("section", None, None),
            P("section", None, None),
            P("section", None, None),
            P("section", None, None),
            P("section", None),
            P("section", None, None),
            P("section", None),
            P(),
        ),
        check_vma=False,
    )
```

profile of v0, /device:TPU:0, one launch (start us, length us, event | category | flops | bytes accessed | tf_op | source)
XLA Modules:
  0.0 2462.7 jit_solution(11942896213256445038)
XLA Ops:
  53.7 119.7 %while.303 = (s32[]{:T(128)}, f32[8,64,64]{2,1,0:T(8,128)}, f32[8,64,64]{2,1,0:T(8,128)}, f32[8,64]{1,0:T(8,128)S(1)}, bf16[2,8,512,64]{2,3,1,0:T(8,128)(2,1)}, ...) while((s32[]{:T(128)}, f32[8,64,64]{2,1,0:T(8,128)}, ...), condition=%wide.region_6.7_spmd.clone, body=%wide.region_2.0_spmd.clone.sunk | while | flops 8867471360 | bytes 118250760 | solution.py:120
  70.9 9.8 fusion.1294
  92.3 8.8 fusion.1298
  127.4 9.8 fusion.1294
  148.9 8.8 fusion.1298
  179.3 11.1 fusion.964
  239.0 119.9 %while.304 = (s32[]{:T(128)}, f32[8,64,64]{2,1,0:T(8,128)}, f32[8,64,64]{2,1,0:T(8,128)}, f32[8,64]{1,0:T(8,128)S(1)}, bf16[2,8,512,64]{2,3,1,0:T(8,128)(2,1)}, ...) while((s32[]{:T(128)}, f32[8,64,64]{2,1,0:T(8,128)}, ...), condition=%wide.region_15.16_spmd.clone, body=%wide.region_11.15_spmd.clone.sunk | while | flops 8867471360 | bytes 118250760 | solution.py:120
  256.1 9.7 fusion.1311
  277.6 8.8 fusion.1315
  312.8 9.7 fusion.1311
  334.2 8.8 fusion.1315
  364.2 12.4 select_select_fusion.4
  485.8 137.0 %while.306 = (s32[]{:T(128)}, f32[8,64,64]{2,1,0:T(8,128)S(1)}, f32[8,64,64]{2,1,0:T(8,128)}, f32[8,64]{1,0:T(8,128)S(1)}, bf16[2,8,512,64]{2,3,1,0:T(8,128)(2,1...) while((s32[]{:T(128)}, f32[8,64,64]{2,1,0:T(8,128)S(1)}, ...), condition=%wide.region_35.36_spmd.clone.clone, body=%wide.region_31.35_spmd.clone.clone.sunk | while | flops 8871997440 | bytes 270655616 | solution.py:120
  498.4 8.9 fusion.1350
  518.6 12.8 bitcast_dynamic-update-slice_fusion.52
  531.4 11.3 fusion.1352
  561.8 8.9 fusion.1350
  581.9 12.8 bitcast_dynamic-update-slice_fusion.52
  594.8 11.3 fusion.1352
  631.9 8.8 fusion.979
  667.9 189.0 %while.307 = (s32[]{:T(128)}, f32[8,64,64]{2,1,0:T(8,128)}, f32[8,64,64]{2,1,0:T(8,128)}, f32[8,64]{1,0:T(8,128)S(1)}, f32[2,8,512,64]{2,3,1,0:T(8,128)}, /*inde...) while((s32[]{:T(128)}, f32[8,64,64]{2,1,0:T(8,128)}, ...), condition=%wide.region_44.45_spmd.clone.clone, body=%wide.region_40.44_spmd.clone.clone.sunk | while | flops 16123170816 | bytes 351799360 | solution.py:120
  676.8 8.9 fusion.1388
  709.2 8.8 fusion.1393
  759.0 8.4 fusion.1387
  767.5 8.9 fusion.1388
  800.0 8.8 fusion.1393
  888.1 9.9 fusion.743
  1026.4 161.3 %while.308 = (s32[]{:T(128)}, f32[8,64,64]{2,1,0:T(8,128)}, f32[8,64,64]{2,1,0:T(8,128)}, f32[8,64]{1,0:T(8,128)S(1)}, bf16[2,8,512,64]{2,3,1,0:T(8,128)(2,1)}, ...) while((s32[]{:T(128)}, f32[8,64,64]{2,1,0:T(8,128)}, ...), condition=%wide.region_53.54_spmd.clone.clone, body=%wide.region_49.53_spmd.clone.clone.sunk | while | flops 8871997440 | bytes 246603824 | solution.py:120
  1064.3 8.9 fusion.1419
  1083.7 12.8 bitcast_dynamic-update-slice_fusion.57
  1096.5 11.4 fusion.1421
  1130.7 8.9 fusion.1419
  1150.1 12.8 bitcast_dynamic-update-slice_fusion.57
  1162.9 11.4 fusion.1421
  1269.1 141.1 %while.310 = (s32[]{:T(128)}, f32[8,64,64]{2,1,0:T(8,128)}, f32[8,64,64]{2,1,0:T(8,128)}, f32[8,64]{1,0:T(8,128)S(1)}, bf16[2,8,512,64]{2,3,1,0:T(8,128)(2,1)}, ...) while((s32[]{:T(128)}, f32[8,64,64]{2,1,0:T(8,128)}, ...), condition=%wide.region_71.72_spmd.clone.clone, body=%wide.region_67.71_spmd.clone.clone.sunk | while | flops 8871997440 | bytes 246603824 | solution.py:120
  1287.0 8.9 fusion.1488
  1306.2 12.8 bitcast_dynamic-update-slice_fusion.62
  1319.0 11.4 fusion.1490
  1353.1 8.9 fusion.1488
  1372.4 12.8 bitcast_dynamic-update-slice_fusion.62
  1385.3 11.4 fusion.1490
  1443.6 11.1 fusion.982
  1480.9 187.9 %while.309 = (s32[]{:T(128)}, f32[8,64,64]{2,1,0:T(8,128)}, f32[8,64,64]{2,1,0:T(8,128)}, f32[8,64]{1,0:T(8,128)S(1)}, f32[2,8,512,64]{2,3,1,0:T(8,128)}, /*inde...) while((s32[]{:T(128)}, f32[8,64,64]{2,1,0:T(8,128)}, ...), condition=%wide.region_62.63_spmd.clone.clone, body=%wide.region_58.62_spmd.clone.clone.sunk | while | flops 16123170816 | bytes 352848000 | solution.py:120
  1489.8 8.9 fusion.1457
  1522.3 8.8 fusion.1462
  1579.9 8.9 fusion.1457
  1612.4 8.8 fusion.1462
  1732.2 12.5 fusion.976
  1771.0 187.8 %while.311 = (s32[]{:T(128)}, f32[8,64,64]{2,1,0:T(8,128)}, f32[8,64,64]{2,1,0:T(8,128)}, f32[8,64]{1,0:T(8,128)S(1)}, f32[2,8,512,64]{2,3,1,0:T(8,128)}, /*inde...) while((s32[]{:T(128)}, f32[8,64,64]{2,1,0:T(8,128)}, ...), condition=%wide.region_80.81_spmd.clone.clone, body=%wide.region_76.80_spmd.clone.clone.sunk | while | flops 16123170816 | bytes 352848000 | solution.py:120
  1779.7 9.0 fusion.1526
  1812.3 8.8 fusion.1531
  1861.4 8.4 fusion.1525
  1869.9 8.9 fusion.1526
  1902.5 8.8 fusion.1531
  2019.7 14.6 add_add_fusion
  2034.3 120.1 %while.305 = (s32[]{:T(128)}, f32[8,64,64]{2,1,0:T(8,128)}, f32[8,64,64]{2,1,0:T(8,128)}, f32[8,64]{1,0:T(8,128)S(1)}, bf16[2,8,512,64]{2,3,1,0:T(8,128)(2,1)}, ...) while((s32[]{:T(128)}, f32[8,64,64]{2,1,0:T(8,128)}, ...), condition=%wide.region_24.25_spmd.clone, body=%wide.region_20.24_spmd.clone.sunk | while | flops 8867471360 | bytes 118250760 | solution.py:120
  2051.5 9.8 fusion.1328
  2072.9 8.8 fusion.1332
  2108.1 9.8 fusion.1328
  2129.7 8.8 fusion.1332
  2159.7 11.3 add_select_fusion
  2181.2 43.7 %psum.15 = f32[64]{0:T(128)} all-reduce(f32[64]{0:T(128)S(1)} %fusion.898), channel_id=1, replica_groups=mesh['section'=2,'dp'=4,'rep'=4] {'section','dp','rep'}, use_global_device_ids=true, to_apply=%region_105.106 | all-reduce | flops 64 | bytes 512 | tf_op jit(solution)/shard_map/psum | solution.py:239
  2239.8 184.5 %all-reduce.17.cloned.1.call-done = f32[3412480]{0:T(1024)} async-done(((f32[3412480]{0:T(1024)}), f32[3412480]{0:T(1024)}) %all-reduce.17.cloned.1.call-update) | async-done | bytes 13649936 | tf_op jit(solution)/shard_map/psum | solution.py:262
  2426.2 9.6 fusion.952
  (1992 shorter events, 1551.4 us)
Async XLA Ops:
  7.2 12.5 copy-start
  7.2 2417.1 %all-reduce.17.cloned.1.call-start = ((), (), s32[]{:S(2)}) async-start(), calls=%async_computation | async-start | bytes 27303936 | tf_op jit(solution)/shard_map/psum | solution.py:262
  15.9 348.2 %copy-start.388 = (f32[1,512]{1,0:T(1,128)}, f32[1,512]{1,0:T(1,128)S(1)}, u32[]{:S(2)}) copy-start(f32[1,512]{1,0:T(1,128)S(1)} %add.801) | copy-start | bytes 6148
  17.0 347.2 %copy-start.390 = (f32[1,1,512]{2,1,0:T(1,128)}, f32[1,1,512]{2,1,0:T(1,128)S(1)}, u32[]{:S(2)}) copy-start(f32[1,1,512]{2,1,0:T(1,128)S(1)} %get-tuple-element.5443) | copy-start | bytes 6148
  17.0 392.3 %copy-start.397 = (f32[1,1,512]{2,1,0:T(1,128)}, f32[1,1,512]{2,1,0:T(1,128)S(1)}, u32[]{:S(2)}) copy-start(f32[1,1,512]{2,1,0:T(1,128)S(1)} %get-tuple-element.5444) | copy-start | bytes 6148
  17.0 347.2 %copy-start.319 = (f32[1,1,512]{2,1,0:T(1,128)}, f32[1,1,512]{2,1,0:T(1,128)S(1)}, u32[]{:S(2)}) copy-start(f32[1,1,512]{2,1,0:T(1,128)S(1)} %get-tuple-element.5441) | copy-start | bytes 6148
  17.0 392.2 %copy-start.305 = (f32[1,1,512]{2,1,0:T(1,128)}, f32[1,1,512]{2,1,0:T(1,128)S(1)}, u32[]{:S(2)}) copy-start(f32[1,1,512]{2,1,0:T(1,128)S(1)} %get-tuple-element.5442) | copy-start | bytes 6148
  176.1 188.1 %copy-start.375 = (f32[1,2048]{1,0:T(1,128)}, f32[1,2048]{1,0:T(1,128)S(1)}, u32[]{:S(2)}) copy-start(f32[1,2048]{1,0:T(1,128)S(1)} %add.800) | copy-start | bytes 24580
  179.3 15.0 copy-start.126
  190.4 5.1 collective-permute-start
  364.2 15.1 copy-start.418
  376.6 20.9 collective-permute-start.1
  498.4 12.4 copy-start.161
  498.4 12.4 copy-start.163
  518.6 12.8 copy-start.53
  518.6 12.8 copy-start.36
  531.4 11.3 copy-start.271
  561.7 12.4 copy-start.161
  561.8 12.4 copy-start.163
  581.9 12.8 copy-start.53
  581.9 12.8 copy-start.36
  594.8 11.3 copy-start.271
  626.7 24.8 %copy-start.332 = (f32[1024]{0:T(1024)}, f32[1024]{0:T(1024)S(1)}, u32[]{:S(2)}) copy-start(f32[1024]{0:T(1024)S(1)} %broadcast_multiply_fusion.5) | copy-start | bytes 12292
  629.0 22.5 copy-start.364
  727.6 12.3 slice-start
  729.9 10.0 slice-start.1
  818.3 12.3 slice-start
  820.6 10.0 slice-start.1
  948.8 492.3 %collective-permute-start.2 = (bf16[1024,512]{0,1:T(8,128)(2,1)}, bf16[1024,512]{0,1:T(8,128)(2,1)}, u32[]{:S(2)}, u32[]{:S(2)}) collective-permute-start(bf16[1024,512]{0,1:T(8,128)(2,1)} %add_convert_fusion.7), channel_id=1, source_target_pairs={{16,0},{17,1},{18,2},{19,3},{20,4},{21,5},{22,6},{23,7},{24,8},{25... | collective-permute-start | bytes 3145736 | tf_op jit(solution)/shard_map/ppermute | solution.py:21
  1064.3 11.5 copy-start.167
  1096.5 11.4 copy-start.72
  1096.5 11.4 copy-start.269
  1096.5 12.5 copy-start.165
  1130.6 11.5 copy-start.167
  1162.9 11.4 copy-start.72
  1162.9 11.4 copy-start.269
  1162.9 12.5 copy-start.165
  1287.0 11.5 copy-start.171
  1319.0 11.4 copy-start.74
  1319.0 11.4 copy-start.267
  1319.0 12.5 copy-start.169
  1353.1 11.5 copy-start.171
  1385.3 11.4 copy-start.74
  1385.3 11.4 copy-start.267
  1385.3 12.5 copy-start.169
  1414.0 20.2 copy-start.137
  1414.0 20.2 copy-start.326
  1414.4 19.9 copy-start.359
  1443.6 11.1 copy-start.177
  1540.0 12.3 slice-start.2
  1542.4 10.0 slice-start.3
  1630.2 12.3 slice-start.2
  1632.5 10.0 slice-start.3
  1716.1 11.1 collective-permute-start.3
  1727.2 17.6 copy-start.188
  1731.0 13.7 copy-start.174
  1732.2 12.5 copy-start.415
  1830.0 12.3 slice-start.4
  1832.3 10.0 slice-start.5
  1920.2 12.3 slice-start.4
  1922.5 10.0 slice-start.5
  2175.7 51.6 %copy-start.367 = (f32[1024]{0:T(1024)S(1)}, f32[1024]{0:T(1024)}, u32[]{:S(2)}) copy-start(f32[1024]{0:T(1024)} %get-tuple-element.4888) | copy-start | bytes 12292
  2175.8 51.7 %copy-start.342 = (f32[1024]{0:T(1024)S(1)}, f32[1024]{0:T(1024)}, u32[]{:S(2)}) copy-start(f32[1024]{0:T(1024)} %copy-done.340) | copy-start | bytes 12292
  2175.8 51.7 %copy-start.356 = (f32[1024]{0:T(1024)S(1)}, f32[1024]{0:T(1024)}, u32[]{:S(2)}) copy-start(f32[1024]{0:T(1024)} %copy-done.355) | copy-start | bytes 12292
  (578 other events, 2176.7 us)
Sparse Core Ops, SparseCore 0:
  2034.4 389.7 all-reduce.16
where the time goes:
time: 2480 us; the launch traced here: 2460 us
  matrix products  1210 us (49%)
  local copies, waits for them, and re-layouts  696 us (28%)
  waiting for transfers between devices  185 us (7%)
  other arithmetic  166 us (7%)
  loops' own time  132 us (5%)
  blocking collectives  43.7 us (2%)
    dot_general x24, matrix products, slot_block(): jnp.einsum('hti,hid->htd', spread_back, value_matrix, precision=running_p...  220 us
    dot_general x24, matrix products, slot_block(): jnp.einsum('htm,him->hti', token_segment_part, softmax_probabilities, pre...  209 us
    dot_general x24, matrix products, slot_block(): jnp.einsum('hti,him->htm', affinity, softmax_probabilities, precision=run...  203 us
    psum x1, waiting for transfers between devices, per_device(): summed = lax.psum(summed, ('dp', 'rep'))  185 us
    dot_general x24, matrix products, slot_block(): jnp.einsum('htd,hid->hti', query_matrix, key_matrix, precision=running_pe...  173 us
    unnamed x550, local copies, waits for them, and re-layouts  140 us
    another operation x9, loops' own time, attend(): ending, (outputs, masses) = lax.scan(slot_block, initial, segment)  132 us
    another operation x69, local copies, waits for them, and re-layouts  112 us
  transfers between devices with their start and end apart: 5, of which 1 were waited for; matrix products, arithmetic and copies ran while one was open for 23% of the time, Pallas kernels for 0%

commit v1 on v0

v1 whole, which is shorter than its diff:
```python
import functools

import jax
import jax.numpy as jnp
from jax import lax
from jax.experimental import pallas as pl
from jax.experimental.pallas import tpu as pltpu
from jax.sharding import PartitionSpec as P

HEADS = 8
DH = 64
SLOTS = 64
LEN = 1024
D = 512
FF = 2048
PAIRS = HEADS // 2
C = 128
ROWS = 256
STEPS = LEN // ROWS
SUBS = ROWS // C
BACK_STEPS = 2
EPSILON = 1e-05
F32 = jnp.float32
BF16 = jnp.bfloat16
GC = 0.7978845608028654
GA = 0.044715
VMEM_LIMIT = 58 * 1024 * 1024

NN = (((1,), (0,)), ((), ()))
NT = (((1,), (1,)), ((), ()))
TN = (((0,), (0,)), ((), ()))


def mm(a, b, dims=NN):
    return lax.dot_general(a, b, dims, preferred_element_type=F32)


def lane_is_low(shape):
    return lax.broadcasted_iota(jnp.int32, shape, 1) % (2 * DH) < DH


def stack_heads(x):
    low = lane_is_low(x.shape)
    zero = jnp.zeros_like(x)
    return jnp.concatenate([jnp.where(low, x, zero), jnp.where(low, zero, x)], axis=0)


def unstack_heads(y):
    half = y.shape[0] // 2
    return jnp.where(lane_is_low((half, y.shape[1])), y[:half], y[half:])


def causal_pair():
    t = lax.broadcasted_iota(jnp.int32, (C, 2 * C), 0)
    i = lax.broadcasted_iota(jnp.int32, (C, 2 * C), 1) % C
    return t >= i


def block_diag_mask():
    a = lax.broadcasted_iota(jnp.int32, (2 * DH, 2 * DH), 0) // DH
    b = lax.broadcasted_iota(jnp.int32, (2 * DH, 2 * DH), 1) // DH
    return a == b


def half_max(x):
    low = lane_is_low(x.shape)
    m0 = jnp.max(jnp.where(low, x, -jnp.inf), axis=-1, keepdims=True)
    m1 = jnp.max(jnp.where(low, -jnp.inf, x), axis=-1, keepdims=True)
    return jnp.where(low, m0, m1)


def half_sum(x):
    low = lane_is_low(x.shape)
    m0 = jnp.sum(jnp.where(low, x, 0.0), axis=-1, keepdims=True)
    m1 = jnp.sum(jnp.where(low, 0.0, x), axis=-1, keepdims=True)
    return jnp.where(low, m0, m1)


def hat(h):
    center = h - jnp.mean(h, axis=-1, keepdims=True)
    spread = jnp.mean(center * center, axis=-1, keepdims=True)
    r = lax.rsqrt(spread + EPSILON)
    return center * r, r


def norm_back(g_hat, xh, r):
    m1 = jnp.mean(g_hat, axis=-1, keepdims=True)
    m2 = jnp.mean(g_hat * xh, axis=-1, keepdims=True)
    return r * (g_hat - m1 - xh * m2)


def start_weight(is_mine, mine, other, dst, sem):
    @pl.when(is_mine)
    def _():
        pltpu.make_async_copy(mine, dst, sem).start()

    @pl.when(jnp.logical_not(is_mine))
    def _():
        pltpu.make_async_copy(other, dst, sem).start()


def wait_weight(mine, dst, sem):
    pltpu.make_async_copy(mine, dst, sem).wait()


V_GAIN1, V_GAIN2, V_BIAS1, V_BIAS2, V_OUTB, V_INB = 0, 1, 2, 3, 4, 5
VROWS = 16


def in_bias_row(vec_ref):
    return jnp.concatenate([vec_ref[V_INB + i : V_INB + i + 1, :] for i in range(4)], axis=1)


def half_ones():
    return block_diag_mask().astype(BF16)


def two_part(x, y, y_first=False):
    high = x.astype(BF16)
    low = (x - high.astype(F32)).astype(BF16)
    if y_first:
        return mm(y, high) + mm(y, low)
    return mm(high, y) + mm(low, y)


def split(x):
    high = x.astype(BF16)
    return high, (x - high.astype(F32)).astype(BF16)


def first_scores(n1, w_in_v, center, n_first, z_first):
    ok = causal_pair()
    tril = (
        lax.broadcasted_iota(jnp.int32, (C, C), 0) >= lax.broadcasted_iota(jnp.int32, (C, C), 1)
    ).astype(BF16)
    qh, ql = split(mm(n1, w_in_v[:, :D]))
    kh, kl = split(mm(n1, w_in_v[:, D : 2 * D]) - center[0:1, :])
    eh, el = split(jnp.exp(mm(n1, w_in_v[:, 3 * D : 4 * D])))
    z_first[...] = mm(tril, eh) + mm(tril, el)
    for p in range(PAIRS):
        cols = slice(p * 128, (p + 1) * 128)
        ks_h, ks_l = stack_heads(kh[:, cols]), stack_heads(kl[:, cols])
        es_h, es_l = stack_heads(eh[:, cols]), stack_heads(el[:, cols])
        aff = mm(qh[:, cols], ks_h, NT) + mm(qh[:, cols], ks_l, NT) + mm(ql[:, cols], ks_h, NT)
        ah, al = split(jnp.where(ok, aff, 0.0))
        n_first[p] = mm(ah, es_h) + mm(al, es_h) + mm(ah, es_l)


def attend_block(first, n_first, z_first, qkve, att, stk_out, stv_out, readout, kst, vst, zst, center, mass):
    ok = causal_pair()
    diag = block_diag_mask()
    ones = half_ones()
    tril = (
        lax.broadcasted_iota(jnp.int32, (C, C), 0) >= lax.broadcasted_iota(jnp.int32, (C, C), 1)
    ).astype(BF16)
    tiles = [(s, p) for s in range(SUBS) for p in range(PAIRS)]

    def rows(s):
        return slice(s * C, (s + 1) * C)

    def part(j, s, p):
        return qkve[rows(s), j * D + p * 128 : j * D + (p + 1) * 128]

    aff, add_k, add_v = {}, {}, {}
    for s, p in tiles:
        aff[s, p] = jnp.where(ok, mm(part(0, s, p), stack_heads(part(1, s, p)), NT), 0.0).astype(BF16)
    for s, p in tiles:
        e = part(3, s, p)
        add_k[s, p] = mm(part(1, s, p), e, TN)
        add_v[s, p] = mm(e, part(2, s, p), TN)
    z_rows = {}
    z_last = zst[...]
    for s in range(SUBS):
        z = mm(tril, qkve[rows(s), 3 * D : 4 * D]) + z_last
        if s == 0:
            z = jnp.where(first, z_first[...], z)
        z_last = z[C - 1 : C, :]
        z_rows[s] = 1.0 / z
        att[1, rows(s), :] = z_rows[s]
    zst[...] = z_last
    for p in range(PAIRS):
        k_run, v_run = kst[p], vst[p]
        for s in range(SUBS):
            stk_out[s, p] = k_run.astype(BF16)
            stv_out[s, p] = v_run.astype(BF16)
            k_run = k_run + jnp.where(diag, add_k[s, p], 0.0)
            v_run = v_run + jnp.where(diag, add_v[s, p], 0.0)
        kst[p], vst[p] = k_run, v_run
    weights = {}
    for s, p in tiles:
        cols = slice(p * 128, (p + 1) * 128)
        n = mm(aff[s, p], stack_heads(part(3, s, p))) + mm(part(0, s, p), stk_out[s, p])
        if s == 0:
            n = jnp.where(first, n_first[p], n)
        rz = z_rows[s][:, cols]
        score = n * rz
        raised = jnp.exp(score - half_max(score))
        prob = raised / two_part(raised, ones)
        w = (prob * rz).astype(BF16)
        weights[s, p] = w
        att[0, rows(s), cols] = prob
        att[2, rows(s), cols] = score
        mass[:, cols] += jnp.sum(prob, axis=0, keepdims=True)
    spread = {}
    for s, p in tiles:
        spread[s, p] = jnp.where(ok, mm(weights[s, p], stack_heads(part(3, s, p)), NT), 0.0).astype(BF16)
    for s, p in tiles:
        cols = slice(p * 128, (p + 1) * 128)
        o = mm(spread[s, p], stack_heads(part(2, s, p))) + mm(weights[s, p], stv_out[s, p])
        readout[rows(s), cols] = (o + center[1:2, cols]).astype(BF16)


def forward_front(first, h, vec, w_in_v, w_out_v, n1_out, qkve, att, stk_out, stv_out, readout, kst, vst, zst, center, firsts, mass,
                  wait_in, wait_out):
    @pl.when(first)
    def _():
        kst[...] = jnp.zeros_like(kst)
        vst[...] = jnp.zeros_like(vst)
        zst[...] = jnp.zeros_like(zst)
        mass[...] = jnp.zeros_like(mass)

    xh, _ = hat(h)
    n1 = (xh * vec[V_GAIN1 : V_GAIN1 + 1, :] + vec[V_BIAS1 : V_BIAS1 + 1, :]).astype(BF16)
    n1_out[...] = n1
    wait_in()
    qkve[:, :D] = mm(n1, w_in_v[:, :D]).astype(BF16)
    for j in (1, 2):
        part = mm(n1, w_in_v[:, j * D : (j + 1) * D])

        @pl.when(first)
        def _(j=j, part=part):
            center[j - 1 : j, :] = jnp.mean(part, axis=0, keepdims=True)

        qkve[:, j * D : (j + 1) * D] = (part - center[j - 1 : j, :]).astype(BF16)
    qkve[:, 3 * D : 4 * D] = jnp.exp(mm(n1, w_in_v[:, 3 * D : 4 * D])).astype(BF16)
    @pl.when(first)
    def _():
        first_scores(n1[:C], w_in_v, center, *firsts)

    attend_block(first, *firsts, qkve, att, stk_out, stv_out, readout, kst, vst, zst, center, mass)
    wait_out()
    return h + mm(readout[...], w_out_v[...])


def gelu_both(x):
    x2 = x * x
    t = jnp.tanh(GC * x * (1.0 + GA * x2))
    half = 0.5 * (1.0 + t)
    return x * half, half + 0.5 * x * (1.0 - t * t) * (GC * (1.0 + 3.0 * GA * x2))


def fwd0_kernel(ids, x, vec, wi_m, wi_o, wo_m, wo_o, wu_m, wu_o, wd_m, wd_o,
                out, n1_out, qkve, att, stk_out, stv_out, readout, middle_out, n2_out, act_out, dgl_out, mass,
                wi_v, wo_v, wu_v, wd_v, kst, vst, zst, center, n_first, z_first, sems):
    c = pl.program_id(0)
    first = c == 0

    @pl.when(first)
    def _():
        mine = ids[0] == 0
        start_weight(mine, wi_m, wi_o, wi_v, sems.at[0])
        start_weight(mine, wo_m, wo_o, wo_v, sems.at[1])
        start_weight(mine, wu_m, wu_o, wu_v, sems.at[2])
        start_weight(mine, wd_m, wd_o, wd_v, sems.at[3])

    def waiter(ref, v, i):
        def go():
            @pl.when(first)
            def _():
                wait_weight(ref, v, sems.at[i])
        return go

    h = x[...].astype(F32)
    middle = forward_front(first, h, vec, wi_v, wo_v, n1_out, qkve, att, stk_out, stv_out, readout, kst, vst, zst,
                           center, (n_first, z_first), mass, waiter(wi_m, wi_v, 0), waiter(wo_m, wo_v, 1))
    middle_out[...] = middle
    xh, _ = hat(middle)
    n2 = (xh * vec[V_GAIN2 : V_GAIN2 + 1, :] + vec[V_BIAS2 : V_BIAS2 + 1, :]).astype(BF16)
    n2_out[...] = n2
    waiter(wu_m, wu_v, 2)()
    inb = in_bias_row(vec)
    for j in range(4):
        cols = slice(j * D, (j + 1) * D)
        act, dgl = gelu_both(mm(n2, wu_v[:, cols]) + inb[:, cols])
        act_out[:, cols] = act.astype(BF16)
        dgl_out[:, cols] = dgl.astype(BF16)
    waiter(wd_m, wd_v, 3)()
    out[...] = middle + mm(act_out[...], wd_v[...]) + vec[V_OUTB : V_OUTB + 1, :]


def row_block(width, dtype=None):
    return pl.BlockSpec((ROWS, width), lambda c, ids: (c, 0))


def const_block(shape):
    n = len(shape)
    return pl.BlockSpec(shape, lambda c, ids: (0,) * n)


ANY = pl.BlockSpec(memory_space=pl.ANY)


def attention_out_shapes():
    return [
        jax.ShapeDtypeStruct((LEN, D), BF16),
        jax.ShapeDtypeStruct((LEN, 4 * D), BF16),
        jax.ShapeDtypeStruct((3, LEN, D), F32),
        jax.ShapeDtypeStruct((LEN // C, PAIRS, 128, 128), BF16),
        jax.ShapeDtypeStruct((LEN // C, PAIRS, 128, 128), BF16),
    ]


def attention_out_specs():
    return [
        row_block(D),
        row_block(4 * D),
        pl.BlockSpec((3, ROWS, D), lambda c, ids: (0, c, 0)),
        pl.BlockSpec((SUBS, PAIRS, 128, 128), lambda c, ids: (c, 0, 0, 0)),
        pl.BlockSpec((SUBS, PAIRS, 128, 128), lambda c, ids: (c, 0, 0, 0)),
    ]


def attention_scratch():
    return [
        pltpu.VMEM((PAIRS, 128, 128), F32),
        pltpu.VMEM((PAIRS, 128, 128), F32),
        pltpu.VMEM((1, D), F32),
        pltpu.VMEM((2, D), F32),
        pltpu.VMEM((PAIRS, C, 128), F32),
        pltpu.VMEM((C, D), F32),
    ]


def weight_scratch():
    return [
        pltpu.VMEM((D, 4 * D), BF16),
        pltpu.VMEM((D, D), BF16),
        pltpu.VMEM((D, FF), BF16),
        pltpu.VMEM((FF, D), BF16),
    ]


def call(kernel, scalars, grid, operands, in_specs, out_specs, scratch, out_shape, name, flops, num_bytes, deps=(),
         aliases=None):
    first = len(scalars) + len(operands)

    def body(*refs):
        kernel(*refs[:first], *refs[first + len(deps) :])

    return pl.pallas_call(
        body,
        grid_spec=pltpu.PrefetchScalarGridSpec(
            num_scalar_prefetch=len(scalars),
            grid=grid,
            in_specs=list(in_specs) + [ANY] * len(deps),
            out_specs=list(out_specs),
            scratch_shapes=list(scratch),
        ),
        out_shape=list(out_shape),
        input_output_aliases=aliases or {},
        compiler_params=params(),
        cost_estimate=pl.CostEstimate(flops=int(flops), bytes_accessed=int(num_bytes), transcendentals=0),
        name=name,
    )(*scalars, *operands, *deps)


def params(**kw):
    return pltpu.CompilerParams(vmem_limit_bytes=VMEM_LIMIT, **kw)


def run_fwd0(ids, inputs, vec, weights, deps=()):
    flat = [w for pair in weights for w in pair]
    return call(
        fwd0_kernel, (ids,), (STEPS,), [inputs, vec, *flat],
        [pl.BlockSpec((ROWS, D), lambda c, ids: (ids[0] * STEPS + c, 0)), const_block((VROWS, D))] + [ANY] * 8,
        [row_block(D)] + attention_out_specs()
            + [row_block(D), row_block(D), row_block(D), row_block(FF), row_block(FF), const_block((1, D))],
        weight_scratch() + attention_scratch() + [pltpu.SemaphoreType.DMA((4,))],
        [jax.ShapeDtypeStruct((LEN, D), F32)] + attention_out_shapes()
        + [
            jax.ShapeDtypeStruct((LEN, D), BF16),
            jax.ShapeDtypeStruct((LEN, D), F32),
            jax.ShapeDtypeStruct((LEN, D), BF16),
            jax.ShapeDtypeStruct((LEN, FF), BF16),
            jax.ShapeDtypeStruct((LEN, FF), BF16),
            jax.ShapeDtypeStruct((1, D), F32),
        ],
        "forward0", 15000000000.0, 33000000.0, deps)


def ffn_back(go, middle, act, dgl, vec, wo_v, wu_v, wd_v, small):
    go_low = go.astype(BF16)
    inner_cols = []
    for j in range(4):
        cols = slice(j * D, (j + 1) * D)
        d_in = mm(go_low, wd_v[cols, :], NT) * dgl[:, cols].astype(F32)
        small[V_INB + j : V_INB + j + 1, :] += jnp.sum(d_in, axis=0, keepdims=True)
        inner_cols.append(d_in.astype(BF16))
    inner_low = jnp.concatenate(inner_cols, axis=1)
    small[V_OUTB : V_OUTB + 1, :] += jnp.sum(go, axis=0, keepdims=True)
    g2 = mm(inner_low, wu_v[...], NT)
    xh, r = hat(middle)
    small[V_GAIN2 : V_GAIN2 + 1, :] += jnp.sum(g2 * xh, axis=0, keepdims=True)
    small[V_BIAS2 : V_BIAS2 + 1, :] += jnp.sum(g2, axis=0, keepdims=True)
    g_mid = go + norm_back(g2 * vec[V_GAIN2 : V_GAIN2 + 1, :], xh, r)
    mid_low = g_mid.astype(BF16)
    return go_low, g_mid, inner_low, mid_low, mm(mid_low, wo_v[...], NT)


FFN_R = 144


def position(rel, core):
    y, x, far, near = rel & 8, rel & 4, rel & 2, rel & 1
    return jnp.where(core == 1, y | (near * 4) | far | (x // 4), (x * 2) | (y // 2) | far | near)


def cost(flops, num_bytes):
    return pl.CostEstimate(flops=int(flops), bytes_accessed=int(num_bytes), transcendentals=0)


def emit_ffn_grads(ids, n2_all, inner_all, act_all, go_all, rd_all, mid_all, keep, send):
    sec, code = ids[0], ids[1]
    for t, dst in ((1, send), (0, keep)):
        half = jnp.where(sec == t, 0, 1)
        spot = [position(j ^ code, half) for j in range(16)]
        n2h = n2_all[:, pl.ds(pl.multiple_of(half * 256, 256), 256)]
        acc = mm(n2h, inner_all[...], TN)
        for j in range(16):
            for cg in range(4):
                dst[spot[j], cg * 16 : (cg + 1) * 16, :] = acc[j * 16 : (j + 1) * 16, cg * 512 : (cg + 1) * 512].astype(BF16)
        rdh = rd_all[:, pl.ds(pl.multiple_of(half * 256, 256), 256)]
        acc = mm(rdh, mid_all[...], TN)
        for j in range(16):
            dst[spot[j], 64:80, :] = acc[j * 16 : (j + 1) * 16, :].astype(BF16)
        acth = act_all[:, pl.ds(pl.multiple_of(half * 1024, 1024), 1024)]
        acc = mm(acth, go_all[...], TN)
        for j in range(16):
            dst[spot[j], 80:144, :] = acc[j * 64 : (j + 1) * 64, :].astype(BF16)


def fwd1_kernel(ids, wseq, x, cot, vec, wi_m, wi_o, wo_m, wo_o, wu_m, wu_o, wd_m, wd_o,
                out, n1_out, qkve, att, stk_out, stv_out, gmid_out, do_out, mass, small, keep, send,
                wi_v, wo_v, wu_v, wd_v, kst, vst, zst, center, n_first, z_first, rd_all, n2_all, act_all, inner_all, go_all, mid_all, dgl_v, sems):
    c = pl.program_id(0)
    first = c == 0

    @pl.when(first)
    def _():
        mine = ids[0] == 1
        start_weight(mine, wi_m, wi_o, wi_v, sems.at[0])
        start_weight(mine, wo_m, wo_o, wo_v, sems.at[1])
        start_weight(mine, wu_m, wu_o, wu_v, sems.at[2])
        start_weight(mine, wd_m, wd_o, wd_v, sems.at[3])
        small[...] = jnp.zeros_like(small)

    def waiter(ref, v, i):
        def go():
            @pl.when(first)
            def _():
                wait_weight(ref, v, sems.at[i])
        return go

    rows = pl.ds(pl.multiple_of(c * ROWS, ROWS), ROWS)
    h = x[...].astype(BF16).astype(F32)
    readout = rd_all.at[rows, :]
    middle = forward_front(first, h, vec, wi_v, wo_v, n1_out, qkve, att, stk_out, stv_out, readout, kst, vst, zst,
                           center, (n_first, z_first), mass, waiter(wi_m, wi_v, 0), waiter(wo_m, wo_v, 1))
    xh, _ = hat(middle)
    n2 = (xh * vec[V_GAIN2 : V_GAIN2 + 1, :] + vec[V_BIAS2 : V_BIAS2 + 1, :]).astype(BF16)
    n2_all[rows, :] = n2
    waiter(wu_m, wu_v, 2)()
    inb = in_bias_row(vec)
    for j in range(4):
        cols = slice(j * D, (j + 1) * D)
        act, dgl = gelu_both(mm(n2, wu_v[:, cols]) + inb[:, cols])
        act_all[rows, cols] = act.astype(BF16)
        dgl_v[:, cols] = dgl.astype(BF16)
    waiter(wd_m, wd_v, 3)()
    out[...] = middle + mm(act_all[rows, :], wd_v[...]) + vec[V_OUTB : V_OUTB + 1, :]
    go = cot[...].astype(F32) * wseq[0]
    go_low, g_mid, inner_low, mid_low, g_rd = ffn_back(go, middle, act_all, dgl_v, vec, wo_v, wu_v, wd_v, small)
    go_all[rows, :] = go_low
    inner_all[rows, :] = inner_low
    mid_all[rows, :] = mid_low
    gmid_out[...] = g_mid
    do_out[...] = g_rd.astype(BF16)

    @pl.when(c == STEPS - 1)
    def _():
        emit_ffn_grads(ids, n2_all, inner_all, act_all, go_all, rd_all, mid_all, keep, send)


def run_fwd1(ids, wseq, out0, cot, vec, weights, deps=()):
    flat = [w for pair in weights for w in pair]
    return call(
        fwd1_kernel, (ids, wseq), (STEPS,), [out0, cot, vec, *flat],
        [
                pl.BlockSpec((ROWS, D), lambda c, ids, w: (c, 0)),
                pl.BlockSpec((ROWS, D), lambda c, ids, w: (ids[0] * STEPS + c, 0)),
                pl.BlockSpec((VROWS, D), lambda c, ids, w: (0, 0)),
            ] + [ANY] * 8,
        [two(s) for s in [row_block(D)] + attention_out_specs()
                       + [row_block(D), row_block(D), const_block((1, D)), const_block((VROWS, D)),
                          const_block((16, FFN_R, 512)), const_block((16, FFN_R, 512))]],
        weight_scratch() + attention_scratch() + [
                pltpu.VMEM((LEN, D), BF16),
                pltpu.VMEM((LEN, D), BF16),
                pltpu.VMEM((LEN, FF), BF16),
                pltpu.VMEM((LEN, FF), BF16),
                pltpu.VMEM((LEN, D), BF16),
                pltpu.VMEM((LEN, D), BF16),
                pltpu.VMEM((ROWS, FF), BF16),
                pltpu.SemaphoreType.DMA((4,))],
        [jax.ShapeDtypeStruct((LEN, D), F32)] + attention_out_shapes()
        + [
            jax.ShapeDtypeStruct((LEN, D), F32),
            jax.ShapeDtypeStruct((LEN, D), BF16),
            jax.ShapeDtypeStruct((1, D), F32),
            jax.ShapeDtypeStruct((VROWS, D), F32),
            jax.ShapeDtypeStruct((16, FFN_R, 512), BF16),
            jax.ShapeDtypeStruct((16, FFN_R, 512), BF16),
        ],
        "forward1", 25000000000.0, 33000000.0, deps)


def two(spec):
    old = spec.index_map
    return pl.BlockSpec(spec.block_shape, lambda c, ids, w: old(c, ids))


def ffn0_kernel(ids, go, middle, n2, act, dgl, readout, vec, wo_m, wo_o, wu_m, wu_o, wd_m, wd_o,
                gmid_out, do_out, small, keep, send,
                wo_v, wu_v, wd_v, rd_all, n2_all, act_all, inner_all, go_all, mid_all, sems):
    c = pl.program_id(0)
    first = c == 0

    @pl.when(first)
    def _():
        mine = ids[0] == 0
        start_weight(mine, wd_m, wd_o, wd_v, sems.at[2])
        start_weight(mine, wu_m, wu_o, wu_v, sems.at[1])
        start_weight(mine, wo_m, wo_o, wo_v, sems.at[0])
        small[...] = jnp.zeros_like(small)
        wait_weight(wd_m, wd_v, sems.at[2])
        wait_weight(wu_m, wu_v, sems.at[1])
        wait_weight(wo_m, wo_v, sems.at[0])

    rows = pl.ds(pl.multiple_of(c * ROWS, ROWS), ROWS)
    rd_all[rows, :] = readout[...]
    n2_all[rows, :] = n2[...]
    act_all[rows, :] = act[...]
    go_low, g_mid, inner_low, mid_low, g_rd = ffn_back(go[...].astype(F32), middle[...], act, dgl, vec, wo_v, wu_v, wd_v, small)
    go_all[rows, :] = go_low
    inner_all[rows, :] = inner_low
    mid_all[rows, :] = mid_low
    gmid_out[...] = g_mid
    do_out[...] = g_rd.astype(BF16)

    @pl.when(c == STEPS - 1)
    def _():
        emit_ffn_grads(ids, n2_all, inner_all, act_all, go_all, rd_all, mid_all, keep, send)


def run_ffn0(ids, go, middle, n2, act, dgl, readout, vec, weights, deps=()):
    flat = [w for pair in weights for w in pair]
    return call(
        ffn0_kernel, (ids,), (STEPS,), [go, middle, n2, act, dgl, readout, vec, *flat],
        [row_block(D), row_block(D), row_block(D), row_block(FF), row_block(FF), row_block(D),
                      const_block((VROWS, D))] + [ANY] * 6,
        [row_block(D), row_block(D), const_block((VROWS, D)),
                       const_block((16, FFN_R, 512)), const_block((16, FFN_R, 512))],
        weight_scratch()[1:] + [
                pltpu.VMEM((LEN, D), BF16),
                pltpu.VMEM((LEN, D), BF16),
                pltpu.VMEM((LEN, FF), BF16),
                pltpu.VMEM((LEN, FF), BF16),
                pltpu.VMEM((LEN, D), BF16),
                pltpu.VMEM((LEN, D), BF16),
                pltpu.SemaphoreType.DMA((3,))],
        [
            jax.ShapeDtypeStruct((LEN, D), F32),
            jax.ShapeDtypeStruct((LEN, D), BF16),
            jax.ShapeDtypeStruct((VROWS, D), F32),
            jax.ShapeDtypeStruct((16, FFN_R, 512), BF16),
            jax.ShapeDtypeStruct((16, FFN_R, 512), BF16),
        ],
        "backward_ffn0", 12000000000.0, 27000000.0, deps)


def attend_back_block(qkve, att, stk, stv, do, proj_low, gk, gv, gz):
    t_idx = lax.broadcasted_iota(jnp.int32, (C, 2 * C), 0)
    i_idx = lax.broadcasted_iota(jnp.int32, (C, 2 * C), 1) % C
    ok, ok_t = t_idx >= i_idx, t_idx <= i_idx
    diag = block_diag_mask()
    ones = half_ones()
    triu = (
        lax.broadcasted_iota(jnp.int32, (C, C), 0) <= lax.broadcasted_iota(jnp.int32, (C, C), 1)
    ).astype(BF16)
    tiles = [(s, p) for s in reversed(range(SUBS)) for p in range(PAIRS)]

    def rows(s):
        return slice(s * C, (s + 1) * C)

    def part(j, s, p):
        return qkve[rows(s), j * D + p * 128 : j * D + (p + 1) * 128]

    def pair(ref, s, p):
        return ref[rows(s), p * 128 : (p + 1) * 128]

    gov, u_all, w_all, dz_all, add_k, add_v = {}, {}, {}, {}, {}, {}
    for s, p in tiles:
        gov[s, p] = jnp.where(ok, mm(pair(do, s, p), stack_heads(part(2, s, p)), NT), 0.0).astype(BF16)
    for s, p in tiles:
        cols = slice(p * 128, (p + 1) * 128)
        prob, rz, score = (att[j, rows(s), cols] for j in range(3))
        dw = mm(gov[s, p], stack_heads(part(3, s, p))) + mm(pair(do, s, p), stv[s, p], NT)
        t = prob * (dw * rz)
        d_score = t - prob * two_part(t, ones)
        u_all[s, p] = (d_score * rz).astype(BF16)
        w_all[s, p] = (prob * rz).astype(BF16)
        dz_all[s, p] = -(w_all[s, p].astype(F32) * (dw * rz) + u_all[s, p].astype(F32) * score)
    for s, p in tiles:
        add_k[s, p] = mm(u_all[s, p], part(0, s, p), TN)
        add_v[s, p] = mm(w_all[s, p], pair(do, s, p), TN)
    gk_low, gv_low, dz_sum = {}, {}, {}
    for p in range(PAIRS):
        cols = slice(p * 128, (p + 1) * 128)
        k_run, v_run, z_run = gk[p], gv[p], gz[:, cols]
        for s in reversed(range(SUBS)):
            gk_low[s, p], gv_low[s, p] = k_run.astype(BF16), v_run.astype(BF16)
            k_run = k_run + jnp.where(diag, add_k[s, p], 0.0)
            v_run = v_run + jnp.where(diag, add_v[s, p], 0.0)
            dz_sum[s, p] = two_part(dz_all[s, p], triu, True) + z_run
            z_run = dz_sum[s, p][0:1, :]
        gk[p], gv[p], gz[:, cols] = k_run, v_run, z_run
    for s, p in tiles:
        q, k, v, e = (part(j, s, p) for j in range(4))
        g_o = pair(do, s, p)
        w, u = w_all[s, p], u_all[s, p]
        us, ws, qs, gos = stack_heads(u), stack_heads(w), stack_heads(q), stack_heads(g_o)
        d = jnp.where(ok, mm(u, stack_heads(e), NT), 0.0).astype(BF16)
        dq = mm(d, stack_heads(k)) + mm(u, stk[s, p], NT)
        d_t = jnp.where(ok_t, mm(e, us, NT), 0.0).astype(BF16)
        dk = mm(d_t, qs) + mm(e, gk_low[s, p])
        b_t = jnp.where(ok_t, mm(e, ws, NT), 0.0).astype(BF16)
        dv = mm(b_t, gos) + mm(e, gv_low[s, p])
        a_t = jnp.where(ok_t, mm(k, qs, NT), 0.0).astype(BF16)
        g_t = jnp.where(ok_t, mm(v, gos, NT), 0.0).astype(BF16)
        de = mm(a_t, us) + mm(g_t, ws) + dz_sum[s, p] + mm(v, gv_low[s, p], NT) + mm(k, gk_low[s, p], NT)
        proj_low[rows(s), p * 128 : (p + 1) * 128] = dq.astype(BF16)
        proj_low[rows(s), D + p * 128 : D + (p + 1) * 128] = dk.astype(BF16)
        proj_low[rows(s), 2 * D + p * 128 : 2 * D + (p + 1) * 128] = dv.astype(BF16)
        proj_low[rows(s), 3 * D + p * 128 : 3 * D + (p + 1) * 128] = (de * e.astype(F32)).astype(BF16)


WIN_R = 64


def attn_back_kernel(layer, carried, *refs):
    ids, x, qkve, att, stk, stv, do, gmid, vec, wi_m, wi_o = refs[:11]
    gh_out, proj_low, gk_out, gv_out, gz_out, small, wi_v, gk, gv, gz, sems = refs[-11:]
    first = pl.program_id(0) == 0

    @pl.when(first)
    def _():
        start_weight(ids[0] == layer, wi_m, wi_o, wi_v, sems.at[0])
        if carried:
            gk_in, gv_in, gz_in, small_in = refs[11:15]
            gk[...], gv[...], gz[...], small[...] = gk_in[...], gv_in[...], gz_in[...], small_in[...]
        else:
            for ref in (small, gk, gv, gz):
                ref[...] = jnp.zeros_like(ref)

    attend_back_block(qkve, att, stk, stv, do, proj_low, gk, gv, gz)

    @pl.when(first)
    def _():
        wait_weight(wi_m, wi_v, sems.at[0])

    g1 = mm(proj_low[...], wi_v[...], NT)
    h = x[...].astype(BF16).astype(F32)
    xh, r = hat(h)
    small[V_GAIN1 : V_GAIN1 + 1, :] += jnp.sum(g1 * xh, axis=0, keepdims=True)
    small[V_BIAS1 : V_BIAS1 + 1, :] += jnp.sum(g1, axis=0, keepdims=True)
    gh = gmid[...] + norm_back(g1 * vec[V_GAIN1 : V_GAIN1 + 1, :], xh, r)
    gh_out[...] = gh.astype(gh_out.dtype)
    gk_out[...], gv_out[...], gz_out[...] = gk[...], gv[...], gz[...]


def run_attn_back(layer, top, steps, carry, ids, x, qkve, att, stk, stv, do, gmid, vec, weight, deps=()):
    def back(width):
        return pl.BlockSpec((ROWS, width), lambda c, ids: (top - 1 - c, 0))

    if layer == 0:
        x_spec = pl.BlockSpec((ROWS, D), lambda c, ids: (ids[0] * STEPS + top - 1 - c, 0))
    else:
        x_spec = back(D)
    state = pl.BlockSpec((SUBS, PAIRS, 128, 128), lambda c, ids: (top - 1 - c, 0, 0, 0))
    carry_shapes = [(PAIRS, 128, 128), (PAIRS, 128, 128), (1, D), (VROWS, D)]
    in_specs = [x_spec, back(4 * D), pl.BlockSpec((3, ROWS, D), lambda c, ids: (0, top - 1 - c, 0)),
                state, state, back(D), back(D), const_block((VROWS, D)), ANY, ANY]
    operands = [x, qkve, att, stk, stv, do, gmid, vec, *weight]
    aliases = {}
    if carry is not None:
        gh, proj, *small_carry = carry
        in_specs = in_specs + [const_block(shape) for shape in carry_shapes] + [ANY, ANY]
        operands = operands + small_carry + [gh, proj]
        aliases = {len(operands) - 1: 0, len(operands): 1}
    return call(
        functools.partial(attn_back_kernel, layer, carry is not None), (ids,), (steps,), operands,
        in_specs,
        [back(D), back(4 * D)] + [const_block(shape) for shape in carry_shapes],
        [pltpu.VMEM((D, 4 * D), BF16)] + attention_scratch()[:3] + [pltpu.SemaphoreType.DMA((1,))],
        [
            jax.ShapeDtypeStruct((LEN, D), F32 if layer == 0 else BF16),
            jax.ShapeDtypeStruct((LEN, 4 * D), BF16),
        ] + [jax.ShapeDtypeStruct(shape, F32) for shape in carry_shapes],
        f"backward_attention{layer}", 9e9 * steps / STEPS, 17e6 * steps / STEPS, deps, aliases)


def in_grad_kernel(ids, n1, proj, keep, send):
    sec, code = ids[0], ids[1]
    for t, dst in ((1, send), (0, keep)):
        half = jnp.where(sec == t, 0, 1)
        n1h = n1[:, pl.ds(pl.multiple_of(half * 256, 256), 256)]
        acc = mm(n1h, proj[...], TN)
        for j in range(16):
            spot = position(j ^ code, half)
            for cg in range(4):
                dst[spot, cg * 16 : (cg + 1) * 16, :] = acc[j * 16 : (j + 1) * 16, cg * 512 : (cg + 1) * 512].astype(BF16)


def run_in_grad(ids, n1, proj, deps=()):
    shape = (16, WIN_R, 512)
    return call(
        in_grad_kernel, (ids,), (1,), [n1, proj],
        [const_block((LEN, D)), const_block((LEN, 4 * D))],
        [const_block(shape), const_block(shape)],
        [],
        [jax.ShapeDtypeStruct(shape, BF16)] * 2,
        "in_grad", 2200000000.0, 7000000.0, deps)


def compute(ids, wseq, inputs, cot, vec0, vec1, weights, comm=None):
    step = comm.step if comm else lambda token: ()
    start = comm.start if comm else lambda *a: None

    def attn_back(layer, token, x, qkve, att, stk, stv, do, gmid, vec):
        carry, top = None, STEPS
        while top > 0:
            carry = run_attn_back(layer, top, BACK_STEPS, carry, ids, x, qkve, att, stk, stv, do, gmid, vec, weights[0],
                                  deps=step(token))
            token = carry[5]
            top -= BACK_STEPS
        return carry[0], carry[1], carry[5]

    (out0, n1, qkve, att, stk, stv, rd, mid, n2, act, dgl, mass0) = run_fwd0(ids, inputs, vec0, weights, deps=step(None))
    (out1, n1b, qkveb, attb, stkb, stvb, gmid1, do1, mass1, small1a, *f1) = run_fwd1(
        ids, wseq, out0, cot, vec1, weights, deps=step(mass0))
    start("f1", f1)
    start("outputs", out0, out1)
    gh1, proj1, small1b = attn_back(1, mass1, out0, qkveb, attb, stkb, stvb, do1, gmid1, vec1)
    a1 = run_in_grad(ids, n1b, proj1, deps=step(small1b))
    gmid0, do0, small0a, *f0 = run_ffn0(ids, gh1, mid, n2, act, dgl, rd, vec0, weights[1:], deps=step(a1[0]))
    start("mix", a1, f0)
    gh0, proj0, small0b = attn_back(0, small0a, inputs, qkve, att, stk, stv, do0, gmid0, vec0)
    a0 = run_in_grad(ids, n1, proj0)
    step(a0[0])
    start("a0", a0)
    return (out0, out1, gh0, gh1, mass0 + mass1, small0a + small0b, small1a + small1b, f0, a0, f1, a1)


class Transfers:
    def __init__(self):
        self.active, self.results = [], {}

    def start(self, name, *parts):
        if name == "outputs":
            first, second = parts
            self.results[name] = (first, to_core(first, 0), second, to_core(second, 1))
            return
        self.results[name] = []
        if name == "small":
            self.active.append([sum_small(*parts, self.results[name]), False])
            return
        core = {"0": 0, "1": 1}.get(name[-1])
        phase = sum_phase(parts, core, self.results[name])
        self.active.append([phase, False])

    def step(self, token):
        deps = []
        for entry in reversed(self.active):
            phase, begun = entry
            try:
                deps.extend(phase.send(token if begun else None))
            except StopIteration:
                pass
            entry[1] = True
        return deps

    def finish(self, work):
        ready = []
        for _ in range(12):
            made = work(self.results)
            ready = self.step(ready + ([] if made is None else [made]))


def cores_swap(x):
    return lax.ppermute(x, "section", [(0, 1), (1, 0)])


def to_core(x, core):
    return lax.ppermute(x, "section", [(1 - core, core)])


def exchange(x, axis, by):
    return lax.ppermute(x, axis, [(i, i ^ by) for i in range(lax.axis_size(axis))])


def add_low(*terms):
    total = terms[0].astype(F32)
    for term in terms[1:]:
        total = total + term.astype(F32)
    return total.astype(BF16)


def exchange_by_core(x, *by):
    dp, rep = lax.axis_size("dp"), lax.axis_size("rep")
    pairs = [
        ((s * dp + z) * rep + r, (s * dp + (z ^ by[s][1])) * rep + (r ^ by[s][0]))
        for s in range(2) for z in range(dp) for r in range(rep)
    ]
    return lax.ppermute(x, ("section", "dp", "rep"), pairs)


FIRST = ((1, 0), (2, 0))
SECOND = ((2, 0), (0, 1))
THIRD = ((0, 1), (1, 0))


def after(token, *arrays):
    tokens = token if isinstance(token, list) else [] if token is None else [token]
    if not tokens:
        return arrays
    return lax.optimization_barrier((*arrays, *tokens))[: len(arrays)]


def sum_phase(parts, core, result):
    keep = parts[0][0] if len(parts) == 1 else jnp.concatenate([k for k, _ in parts], axis=1)
    send = parts[0][1] if len(parts) == 1 else jnp.concatenate([s for _, s in parts], axis=1)
    got = cores_swap(send)
    token = yield [keep]
    (got,) = after(token, got)
    away, home = add_low(keep[8:], got[8:]), add_low(keep[:8], got[:8])
    got = exchange_by_core(away, *FIRST)
    token = yield [away, home]
    (got,) = after(token, got)
    away, home = add_low(home[4:], got[4:]), add_low(home[:4], got[:4])
    got = exchange_by_core(away, *SECOND)
    token = yield [away, home]
    (got,) = after(token, got)
    home, got = (x.reshape(2, 2, *x.shape[1:]) for x in (home, got))
    away, home = add_low(home[:, 1], got[:, 1]), add_low(home[:, 0], got[:, 0])
    got = exchange_by_core(away, *THIRD)
    token = yield [away, home]
    (got,) = after(token, got)
    away, home = add_low(home[1], got[1]), add_low(home[0], got[0])
    got = exchange(away, "dp", 2)
    token = yield [away, home]
    (got,) = after(token, got)
    s = add_low(home, got)
    bit = 4
    while bit < lax.axis_size("dp"):
        s = add_low(s, exchange(s, "dp", bit))
        bit *= 2
    got = exchange(s, "dp", 2)
    token = yield [s]
    (got,) = after(token, got)
    s = jnp.stack([s, got])
    got = exchange_by_core(s, *THIRD)
    token = yield [s]
    (got,) = after(token, got)
    s = jnp.stack([s, got], axis=1).reshape(4, *s.shape[1:])
    got = exchange_by_core(s, *SECOND)
    token = yield [s]
    (got,) = after(token, got)
    low = jnp.concatenate([s, got], axis=0)
    high = exchange_by_core(low, *FIRST)
    send_on = cores_swap if core is None else lambda x: to_core(x, core)
    far_low = send_on(low)
    token = yield [low]
    (high,) = after(token, high)
    result.extend([low, high, far_low, send_on(high)])
    yield [high]


def sum_small(x, result):
    for axis in ("section", "rep", "dp"):
        bit = 1
        while bit < lax.axis_size(axis):
            got = exchange(x, axis, bit)
            token = yield [x]
            (got,) = after(token, got)
            x = x + got
            bit *= 2
    result.append(x)
    yield [x]


def pick_source(ids, h, own0, recv0, own1, recv1, body):
    layer_one = ids[0] == 1
    own_half = h == ids[0]
    for src, use in (
        (own0, jnp.logical_and(jnp.logical_not(layer_one), own_half)),
        (recv0, jnp.logical_and(jnp.logical_not(layer_one), jnp.logical_not(own_half))),
        (own1, jnp.logical_and(layer_one, own_half)),
        (recv1, jnp.logical_and(layer_one, jnp.logical_not(own_half))),
    ):
        @pl.when(use)
        def _(src=src):
            body(src)


def source_specs(shape, inner):
    rest = (0,) * (len(shape) - 1)

    def spec(layer, own):
        def index(h, i, ids):
            used = jnp.logical_and(ids[0] == layer, (h == ids[0]) == own)
            return (jnp.where(used, inner(i, ids), 0),) + rest

        return pl.BlockSpec(shape, index)

    return [spec(0, True), spec(0, False), spec(1, True), spec(1, False)]


def unpack_kernel(store, offsets, ids, *refs):
    sources, outs, (buf, sems) = refs[:8], refs[8:-2], refs[-2:]
    sec, code = ids[0], ids[1]
    h = pl.program_id(0)

    def fetch(half, slot, start):
        for k, part in enumerate(sources):
            layer, received, upper = k // 4, (k // 2) % 2, k % 2
            def copy(part=part, upper=upper, layer=layer):
                src = part.at[:, pl.ds(offsets[layer], buf.shape[2]), :]
                return pltpu.make_async_copy(src, buf.at[slot, pl.ds(8 * upper, 8)], sems.at[slot, upper])

            if start:
                @pl.when(jnp.logical_and(sec == layer, (half == sec) == (received == 0)))
                def _(copy=copy):
                    copy().start()
            elif k < 2:
                copy().wait()

    @pl.when(h == 0)
    def _():
        fetch(0, 0, True)
        fetch(1, 1, True)

    fetch(h, h, False)
    for j in range(16):
        store(j, buf.at[h, position(j ^ code, h)], outs)


def store_ffn(j, src, outs):
    up, out, down = outs
    for cg in range(4):
        up[j * 16 : (j + 1) * 16, cg * 512 : (cg + 1) * 512] = src[cg * 16 : (cg + 1) * 16, :].astype(F32)
    out[j * 16 : (j + 1) * 16, :] = src[64:80, :].astype(F32)
    down[j * 64 : (j + 1) * 64, :] = src[80:144, :].astype(F32)


def store_in(j, src, outs):
    for cg in range(4):
        outs[0][j * 16 : (j + 1) * 16, cg * 512 : (cg + 1) * 512] = src[cg * 16 : (cg + 1) * 16, :].astype(F32)


def unpack(ids, sources, store, shapes, rows, offsets, name, deps=()):
    return call(
        functools.partial(unpack_kernel, store, offsets), (ids,), (2,), sources,
        [ANY] * 8,
        [pl.BlockSpec((shape[0] // 2, shape[1]), lambda h, ids: (h, 0)) for shape in shapes],
        [pltpu.VMEM((2, 16, rows, 512), BF16), pltpu.SemaphoreType.DMA((2, 2))],
        [jax.ShapeDtypeStruct(shape, F32) for shape in shapes],
        name, 1000000.0, 3 * 4 * 8192 * rows, deps)


def assemble_kernel(ids, own0, recv0, own1, recv1, out):
    def body(src):
        out[...] = src[...].astype(F32)

    pick_source(ids, pl.program_id(0), own0, recv0, own1, recv1, body)


def assemble(ids, sources, name, deps=()):
    return call(
        assemble_kernel, (ids,), (2, 2), sources,
        source_specs((512, D), lambda i, ids: i),
        [pl.BlockSpec((512, D), lambda h, i, ids: (h * 2 + i, 0))],
        [],
        [jax.ShapeDtypeStruct((2 * LEN, D), F32)],
        name, 1000000.0, 8000000.0, deps)[0]


def pack_vectors(norm_gains, norm_biases, in_bias, out_bias):
    rows = [norm_gains[0], norm_biases[0], out_bias, in_bias.reshape(4, D)]
    used = sum(r.shape[0] for r in rows)
    return jnp.concatenate(rows + [jnp.zeros((VROWS - used, D), BF16)], axis=0)


def per_device(inputs, cotangent, domain_ids, group_of, group_weights, norm_gains, norm_biases,
               w_in, w_out, w_up, in_bias, w_down, out_bias):
    sec = lax.axis_index("section")
    code = lax.axis_index("rep") * 4 + lax.axis_index("dp") % 4
    ids = jnp.stack([sec, code]).astype(jnp.int32)
    leading = sec == 0
    mine = [w_in[0], w_out[0], w_up[0], w_down[0]]
    vec_mine = pack_vectors(norm_gains, norm_biases, in_bias, out_bias)
    vec_other = cores_swap(vec_mine)
    weights = [(w, cores_swap(w)) for w in mine]
    vec0 = jnp.where(leading, vec_mine, vec_other).astype(F32)
    vec1 = jnp.where(leading, vec_other, vec_mine).astype(F32)
    own_id = jnp.where(leading, domain_ids[0], domain_ids[1])
    domain_hit = own_id == jnp.arange(group_of.shape[0])
    group = jnp.sum(jnp.where(domain_hit, group_of, 0))
    wseq = jnp.sum(jnp.where(group == jnp.arange(group_weights.shape[0]), group_weights, 0.0)).reshape(1)

    comm = Transfers()
    (out0, out1, gh0, gh1, mass, small0, small1, *_) = compute(ids, wseq, inputs, cotangent, vec0, vec1, weights, comm)
    made = {}
    comm.results["grads"] = (gh0, to_core(gh0, 0), gh1, to_core(gh1, 1))

    def work(got):
        if "outputs" not in made:
            made["outputs"] = assemble(ids, got["outputs"], "layer_outputs")
            return made["outputs"]
        if "grads" not in made:
            made["grads"] = assemble(ids, got["grads"], "input_grads")
            return made["grads"]
        if "ffn" not in made and got["mix"] and got["f1"]:
            shapes = ((D, FF), (D, D), (FF, D))
            made["ffn"] = unpack(ids, got["mix"] + got["f1"], store_ffn, shapes, FFN_R, (WIN_R, 0), "unpack_ffn")
            return made["ffn"][0]
        return None

    comm.start("small", jnp.concatenate([small0[:9], small1[:9], mass, jnp.zeros((5, D), F32)], axis=0))
    comm.finish(work)
    got = comm.results
    layer_outputs, input_grads = made["outputs"], made["grads"]
    g_up, g_wout, g_down = made["ffn"]
    (g_win,) = unpack(ids, got["a0"] + got["mix"], store_in, ((D, 4 * D),), WIN_R, (0, 0), "unpack_in")

    (total,) = got["small"]
    small = jnp.where(leading, total[:9], total[9:18])
    slot_mass = jnp.sum(total[18].reshape(HEADS, SLOTS), axis=0) / (HEADS * 2 * LEN)
    return (
        layer_outputs[None],
        input_grads[None],
        small[0:2][None],
        small[2:4][None],
        g_win[None],
        g_wout[None],
        g_up[None],
        small[V_INB : V_INB + 4].reshape(1, FF),
        g_down[None],
        small[V_OUTB][None],
        slot_mass,
    )


def solution(mesh):
    return jax.shard_map(
        per_device,
        mesh=mesh,
        in_specs=(
            P(("dp", "rep"), None),
            P(("dp", "rep"), None),
            P(("dp", "rep")),
            P(),
            P(),
            P("section", None, None),
            P("section", None, None),
            P("section", None, None),
            P("section", None, None),
            P("section", None, None),
            P("section", None),
            P("section", None, None),
            P("section", None),
        ),
        out_specs=(
            P("section", ("dp", "rep"), None),
            P("section", ("dp", "rep"), None),
            P("section", None, None),
            P("section", None, None),
            P("section", None, None),
            P("section", None, None),
            P("section", None, None),
            P("section", None),
            P("section", None, None),
            P("section", None),
            P(),
        ),
        check_vma=False,
    )
```

time: 2480 us -> 408 us (0.16)
  matrix products: 1210 us -> 0 us
  local copies, waits for them, and re-layouts: 696 us -> 8.18 us
  Pallas kernels: 0 us -> 218 us
  other arithmetic: 166 us -> 26.3 us
  loops' own time: 132 us -> 0 us
  waiting for transfers between devices: 185 us -> 92.8 us
  blocking collectives: 43.7 us -> 0 us
  starting transfers between devices: 9.16 us -> 51.8 us
    dot_general x252 -> x0, matrix products: 1210 us -> none  [the longest x24 220 us: slot_block(): jnp.einsum('hti,hid->htd', spread_back, value_matrix, precision=running_p...]
    pallas_call x0 -> x13, Pallas kernels: none -> 218 us  [call(): pl.pallas_call(body, grid_spec=pltpu.PrefetchScalarGridSpec(num_scalar_pr...]
    psum x1 -> x0, waiting for transfers between devices: 185 us -> none  [per_device(): summed = lax.psum(summed, ('dp', 'rep'))]
    unnamed x550 -> x77, local copies, waits for them, and re-layouts: 140 us -> 4.44 us
    another operation x9 -> x0, loops' own time: 132 us -> none  [attend(): ending, (outputs, masses) = lax.scan(slot_block, initial, segment)]
    another operation x75 -> x2, local copies, waits for them, and re-layouts: 129 us -> 0.12 us  [the longest x1 0.08 us: per_device(): total[18].reshape(HEADS, SLOTS)]
    slice x50 -> x3, local copies, waits for them, and re-layouts: 109 us -> 1.92 us  [the longest x1 1.31 us: per_device(): own_id = jnp.where(leading, domain_ids[0], domain_ids[1])]
    reduce_sum x67 -> x3, other arithmetic: 102 us -> 3.22 us  [the longest x1 1.91 us: per_device(): jnp.sum(jnp.where(group == jnp.arange(group_weights.shape[0]), group_weig...]
  transfers between devices with their start and end apart: 5 -> 47, of which waited for: 1 -> 20; matrix products, arithmetic and copies ran while one was open for 23% -> 6% of each run, Pallas kernels for 0% -> 26%
where the time goes in v1:
time: 408 us; the launch traced here: 400 us
  Pallas kernels  218 us (53%)
  waiting for transfers between devices  92.8 us (23%)
  starting transfers between devices  51.8 us (13%)
  other arithmetic  26.3 us (6%)
  local copies, waits for them, and re-layouts  8.18 us (2%)
    pallas_call x13, Pallas kernels, call(): pl.pallas_call(body, grid_spec=pltpu.PrefetchScalarGridSpec(num_scalar_pr...  218 us
    ppermute x18, waiting for transfers between devices, exchange_by_core(): return lax.ppermute(x, ('section', 'dp', 'rep'), pairs)  49.6 us
    ppermute x11, waiting for transfers between devices, exchange(): lax.ppermute(x, axis, [(i, i ^ by) for i in range(lax.axis_size(axis))])  40.7 us
    ppermute x8, starting transfers between devices, to_core(): return lax.ppermute(x, 'section', [(1 - core, core)])  18.6 us
    ppermute x18, starting transfers between devices, exchange_by_core(): return lax.ppermute(x, ('section', 'dp', 'rep'), pairs)  16.9 us
    ppermute x11, starting transfers between devices, exchange(): lax.ppermute(x, axis, [(i, i ^ by) for i in range(lax.axis_size(axis))])  14.4 us
    convert_element_type x15, other arithmetic, add_low(): return total.astype(BF16)  14.4 us
  transfers between devices with their start and end apart: 47, of which 20 were waited for; matrix products, arithmetic and copies ran while one was open for 6% of the time, Pallas kernels for 26%

profile of v1, /device:TPU:0, one launch (start us, length us, event | category | flops | bytes accessed | tf_op | source)
XLA Modules:
  0.0 400.2 jit_solution(11962655637036620514)
XLA Ops:
  3.8 1.3 fusion.20
  6.5 1.3 fusion.15
  7.8 1.9 fusion.16
  10.9 1.2 collective-permute-done.4.refs_10_.refs_12_.refs_13_
  12.4 36.7 %forward0.1 = (f32[1024,512]{1,0:T(8,128)}, bf16[1024,512]{1,0:T(8,128)(2,1)}, bf16[1024,2048]{1,0:T(8,128)(2,1)}, f32[3,1024,512]{2,1,0:T(8,128)}, bf16[8,4,128...) custom-call(s32[2]{0:T(128)} %pad_add_fusion.refs_0_, ...), custom_call_target="tpu_custom_call" | custom-call | flops 15000000512 | bytes 33000000 | tf_op jit(solution)/shard_map/forward0/pallas_call | solution.py:350
  49.0 50.5 %forward1.1 = (f32[1024,512]{1,0:T(8,128)}, bf16[1024,512]{1,0:T(8,128)(2,1)}, bf16[1024,2048]{1,0:T(8,128)(2,1)}, f32[3,1024,512]{2,1,0:T(8,128)}, bf16[8,4,128...) custom-call(s32[2]{0:T(128)} %pad_add_fusion.refs_0_, ...), custom_call_target="tpu_custom_call" | custom-call | flops 24999999488 | bytes 33000000 | tf_op jit(solution)/shard_map/forward1/pallas_call | solution.py:350
  99.7 17.9 %backward_attention1.2 = (bf16[1024,512]{1,0:T(8,128)(2,1)}, bf16[1024,2048]{1,0:T(8,128)(2,1)}, f32[4,128,128]{2,1,0:T(8,128)}, f32[4,128,128]{2,1,0:T(8,128)}, f32[1,512]{1,0:T(1,128)}, /*index=5*/f32[16,512]{1,0:T(8,128)}) custom-call(s32[2]{0:T(128)} %pad_add_fusion.refs_0_, f32[1024,512]{1,0:T(8,128)} %get-tuple-element.97.refs_2_.refs_1_, ...), custom_call_target="tpu_custom_call" | custom-call | flops 4499999744 | bytes 8500000 | tf_op jit(solution)/shard_map/backward_attention1/pallas_call | solution.py:350
  117.7 1.8 add_convert_fusion.2
  119.5 2.9 collective-permute-start.8
  122.4 18.6 %backward_attention1.3 = (bf16[1024,512]{1,0:T(8,128)(2,1)}, bf16[1024,2048]{1,0:T(8,128)(2,1)}, f32[4,128,128]{2,1,0:T(8,128)}, f32[4,128,128]{2,1,0:T(8,128)}, f32[1,512]{1,0:T(1,128)}, /*index=5*/f32[16,512]{1,0:T(8,128)}) custom-call(s32[2]{0:T(128)} %pad_add_fusion.refs_0_, ...), custom_call_target="tpu_custom_call", output_to_operand_aliasing={{0}: (15, {}), {1}: (16, {})} | custom-call | flops 4499999744 | bytes 8500000 | tf_op jit(solution)/shard_map/backward_attention1/pallas_call | solution.py:350
  141.0 1.1 add_convert_fusion.7
  142.2 1.5 collective-permute-start.9
  143.7 6.7 %in_grad.2 = (bf16[16,64,512]{2,1,0:T(8,128)(2,1)}, bf16[16,64,512]{2,1,0:T(8,128)(2,1)}) custom-call(s32[2]{0:T(128)} %pad_add_fusion.refs_0_, bf16[1024,512]{1,0:T(8,128)(2,1)} %get-tuple-element.126.refs_1_, bf16[1024,2048]{1,0:T(8,128)(2,1)} %get-tuple-element.127.refs_2_, bf16[4,144,512]{2,1,0:T(8,128)(2,1)} %copy-done.24, ...), custom_call_target="tpu_custom_call" | custom-call | flops 2200000000 | bytes 7000000 | tf_op jit(solution)/shard_map/in_grad/pallas_call | solution.py:350
  150.4 1.6 collective-permute-done.9
  153.0 21.1 %backward_ffn0.1 = (f32[1024,512]{1,0:T(8,128)}, bf16[1024,512]{1,0:T(8,128)(2,1)}, f32[16,512]{1,0:T(8,128)}, bf16[16,144,512]{2,1,0:T(8,128)(2,1)}, bf16[16,144,512]{2,1,0:T(8,128)(2,1)}) custom-call(s32[2]{0:T(128)} %pad_add_fusion.refs_0_, bf16[1024,512]{1,0:T(8,128)(2,1)} %get-tuple-element.118.refs_1_.refs_3_, f32[1024,512]{1,0:T(8,128)} %get-tuple-element.119.refs_2_, ...), custom_call_target="tpu_custom_call" | custom-call | flops 12000000000 | bytes 27000000 | tf_op jit(solution)/shard_map/backward_ffn0/pallas_call | solution.py:350
  174.2 3.8 pad_maximum_fusion
  178.0 1.3 collective-permute-start.5
  179.3 5.7 %collective-permute-start.6 = (f32[1024,512]{1,0:T(8,128)}, f32[1024,512]{1,0:T(8,128)}, u32[]{:S(2)}, u32[]{:S(2)}) collective-permute-start(f32[1024,512]{1,0:T(8,128)} %get-tuple-element.98.refs_3_), channel_id=1, source_target_pairs={{0,16},{1,17},{2,18},{3,19},{4,20},{5,21},{6,22},{7,23},{8,24},{9,... | collective-permute-start | bytes 6291464 | tf_op jit(solution)/shard_map/ppermute | solution.py:814
  185.1 1.6 collective-permute-start.10
  187.0 4.8 %collective-permute-done.10 = bf16[2,144,512]{2,1,0:T(8,128)(2,1)S(1)} collective-permute-done((bf16[2,144,512]{2,1,0:T(8,128)(2,1)S(1)}, bf16[2,144,512]{2,1,0:T(8,128)(2,1)S(1)}, u32[]{:S(2)}, u32[]{:S(2)}) %collective-permute-start.10) | collective-permute-done | bytes 294944 | tf_op jit(solution)/shard_map/ppermute | solution.py:834
  192.6 2.6 collective-permute-start.12
  195.2 18.1 %backward_attention0.2 = (f32[1024,512]{1,0:T(8,128)}, bf16[1024,2048]{1,0:T(8,128)(2,1)}, f32[4,128,128]{2,1,0:T(8,128)}, f32[4,128,128]{2,1,0:T(8,128)}, f32[1,512]{1,0:T(1,128)}, /*index=5*/f32[16,512]{1,0:T(8,128)}) custom-call(s32[2]{0:T(128)} %pad_add_fusion.refs_0_, bf16[2048,512]{1,0:T(8,128)(2,1)} %refs_1_.5, ...), custom_call_target="tpu_custom_call" | custom-call | flops 4499999744 | bytes 8500000 | tf_op jit(solution)/shard_map/backward_attention0/pallas_call | solution.py:350
  213.2 5.3 %add_convert_fusion = (bf16[8,208,512]{2,1,0:T(8,128)(2,1)}, bf16[8,208,512]{2,1,0:T(8,128)(2,1)S(1)}) fusion(bf16[16,208,512]{2,1,0:T(8,128)(2,1)} %copy-done.2, bf16[16,208,512]{2,1,0:T(8,128)(2,1)} %collective-permute-done.11), kind=kLoop, calls=%fused_computation.1 | loop fusion | flops 6815744 | bytes 10223616 | tf_op jit(solution)/shard_map/convert_element_type | solution.py:825
  220.3 18.5 %backward_attention0.3 = (f32[1024,512]{1,0:T(8,128)}, bf16[1024,2048]{1,0:T(8,128)(2,1)}, f32[4,128,128]{2,1,0:T(8,128)}, f32[4,128,128]{2,1,0:T(8,128)}, f32[1,512]{1,0:T(1,128)}, /*index=5*/f32[16,512]{1,0:T(8,128)}) custom-call(s32[2]{0:T(128)} %pad_add_fusion.refs_0_, ...), custom_call_target="tpu_custom_call", output_to_operand_aliasing={{0}: (15, {}), {1}: (16, {})} | custom-call | flops 4499999744 | bytes 8500000 | tf_op jit(solution)/shard_map/backward_attention0/pallas_call | solution.py:350
  238.8 1.3 collective-permute-start.13
  240.8 6.7 %in_grad.3 = (bf16[16,64,512]{2,1,0:T(8,128)(2,1)}, bf16[16,64,512]{2,1,0:T(8,128)(2,1)}) custom-call(s32[2]{0:T(128)} %pad_add_fusion.refs_0_, bf16[1024,512]{1,0:T(8,128)(2,1)} %get-tuple-element.150.refs_1_, bf16[1024,2048]{1,0:T(8,128)(2,1)} %get-tuple-element.151.refs_2_), custom_call_target="tpu_custom_call" | custom-call | flops 2200000000 | bytes 7000000 | tf_op jit(solution)/shard_map/in_grad/pallas_call | solution.py:350
  247.5 2.2 collective-permute-done.18
  249.7 3.9 collective-permute-start.14
  254.9 2.8 add_convert_fusion.5
  257.7 1.5 collective-permute-start.17
  259.3 6.7 %layer_outputs.1 = f32[2048,512]{1,0:T(8,128)} custom-call(s32[2]{0:T(128)} %pad_add_fusion.refs_0_, f32[1024,512]{1,0:T(8,128)} %get-tuple-element.97.refs_2_.refs_1_, f32[1024,512]{1,0:T(8,128)} %collective-permute-done.5.refs_2_, f32[1024,512]{1,0:T(8,128)} %get-tuple-element.98.refs_3_, f32[1024,512]{1,0:T(8,128)} %collective-permute-done.6.refs_4_), custom_call_target="tpu_custom_call" | custom-call | flops 1000000 | bytes 8000000 | tf_op jit(solution)/shard_map/layer_outputs/pallas_call | solution.py:350
  267.9 6.1 %input_grads.1 = f32[2048,512]{1,0:T(8,128)} custom-call(s32[2]{0:T(128)} %pad_add_fusion.refs_0_, f32[1024,512]{1,0:T(8,128)} %get-tuple-element.145.refs_1_, f32[1024,512]{1,0:T(8,128)} %collective-permute-done.13.refs_2_, bf16[1024,512]{1,0:T(8,128)(2,1)} %get-tuple-element.118.refs_1_.refs_3_, bf16[1024,512]{1,0:T(8,128)(2,1)} %collective-permute-done.14.refs_4_), custom_call_target="tpu_custom_call" | custom-call | flops 1000000 | bytes 8000000 | tf_op jit(solution)/shard_map/input_grads/pallas_call | solution.py:350
  274.2 1.6 collective-permute-start.22
  275.8 1.4 collective-permute-done.23
  278.6 1.1 collective-permute-start.25
  279.8 2.6 collective-permute-done.22
  282.5 2.3 collective-permute-start.26
  284.8 1.2 collective-permute-done.15
  286.1 1.0 collective-permute-start.20
  287.1 14.5 %collective-permute-done.20 = f32[24,512]{1,0:T(8,128)S(1)} collective-permute-done((f32[24,512]{1,0:T(8,128)S(1)}, f32[24,512]{1,0:T(8,128)S(1)}, u32[]{:S(2)}, u32[]{:S(2)}) %collective-permute-start.20) | collective-permute-done | bytes 49184 | tf_op jit(solution)/shard_map/ppermute | solution.py:818
  301.7 1.2 collective-permute-start.30
  303.0 1.1 collective-permute-start.29
  304.1 6.7 %collective-permute-done.30 = bf16[208,512]{1,0:T(8,128)(2,1)S(1)} collective-permute-done((bf16[208,512]{1,0:T(8,128)(2,1)S(1)}, bf16[208,512]{1,0:T(8,128)(2,1)S(1)}, u32[]{:S(2)}, u32[]{:S(2)}) %collective-permute-start.30) | collective-permute-done | bytes 213024 | tf_op jit(solution)/shard_map/ppermute | solution.py:818
  311.0 1.5 collective-permute-start.24
  312.5 2.7 collective-permute-done.24
  315.2 6.5 %collective-permute-done.33 = bf16[2,208,512]{2,1,0:T(8,128)(2,1)S(1)} collective-permute-done((bf16[2,208,512]{2,1,0:T(8,128)(2,1)S(1)}, bf16[2,208,512]{2,1,0:T(8,128)(2,1)S(1)}, u32[]{:S(2)}, u32[]{:S(2)}) %collective-permute-start.33) | collective-permute-done | bytes 426016 | tf_op jit(solution)/shard_map/ppermute | solution.py:834
  322.0 2.0 collective-permute-start.28
  324.0 5.5 %collective-permute-done.28 = f32[24,512]{1,0:T(8,128)S(1)} collective-permute-done((f32[24,512]{1,0:T(8,128)S(1)}, f32[24,512]{1,0:T(8,128)S(1)}, u32[]{:S(2)}, u32[]{:S(2)}) %collective-permute-start.28) | collective-permute-done | bytes 49184 | tf_op jit(solution)/shard_map/ppermute | solution.py:818
  329.5 5.6 %collective-permute-done.36 = bf16[4,208,512]{2,1,0:T(8,128)(2,1)S(1)} collective-permute-done((bf16[4,208,512]{2,1,0:T(8,128)(2,1)S(1)}, bf16[4,208,512]{2,1,0:T(8,128)(2,1)S(1)}, u32[]{:S(2)}, u32[]{:S(2)}) %collective-permute-start.36) | collective-permute-done | bytes 852000 | tf_op jit(solution)/shard_map/ppermute | solution.py:834
  336.3 2.9 collective-permute-start.31
  339.2 2.2 collective-permute-done.34
  342.1 15.0 %collective-permute-done.38.refs_2_.refs_6_ = bf16[8,208,512]{2,1,0:T(8,128)(2,1)S(1)} collective-permute-done((bf16[8,208,512]{2,1,0:T(8,128)(2,1)S(1)}, bf16[8,208,512]{2,1,0:T(8,128)(2,1)S(1)}, u32[]{:S(2)}, u32[]{:S(2)}) %collective-permute-start.38) | collective-permute-done | bytes 1703968 | tf_op jit(solution)/shard_map/ppermute | solution.py:834
  357.2 2.5 collective-permute-start.41
  359.6 1.4 collective-permute-start.42
  361.1 5.2 %collective-permute-done.35 = bf16[64,512]{1,0:T(8,128)(2,1)S(1)} collective-permute-done((bf16[64,512]{1,0:T(8,128)(2,1)S(1)}, bf16[64,512]{1,0:T(8,128)(2,1)S(1)}, u32[]{:S(2)}, u32[]{:S(2)}) %collective-permute-start.35) | collective-permute-done | bytes 65568 | tf_op jit(solution)/shard_map/ppermute | solution.py:818
  367.8 1.2 copy-done.8
  368.9 6.2 %unpack_ffn.1 = (f32[512,2048]{1,0:T(8,128)}, f32[512,512]{1,0:T(8,128)}, f32[2048,512]{1,0:T(8,128)}) custom-call(s32[2]{0:T(128)} %pad_add_fusion.refs_0_, bf16[8,208,512]{2,1,0:T(8,128)(2,1)} %copy-done.3, bf16[8,208,512]{2,1,0:T(8,128)(2,1)} %copy-done.7, bf16[8,208,512]{2,1,0:T(8,128)(2,1)} %copy-done.8, ...), custom_call_target="tpu_custom_call" | custom-call | flops 1000000 | bytes 14155776 | tf_op jit(solution)/shard_map/unpack_ffn/pallas_call | solution.py:350
  375.3 6.4 %collective-permute-done.43 = bf16[4,64,512]{2,1,0:T(8,128)(2,1)S(1)} collective-permute-done((bf16[4,64,512]{2,1,0:T(8,128)(2,1)S(1)}, bf16[4,64,512]{2,1,0:T(8,128)(2,1)S(1)}, u32[]{:S(2)}, u32[]{:S(2)}) %collective-permute-start.43) | collective-permute-done | bytes 262176 | tf_op jit(solution)/shard_map/ppermute | solution.py:834
  381.7 1.0 collective-permute-start.44
  384.0 1.3 collective-permute-start.45
  385.3 5.7 %collective-permute-done.44.refs_2_ = bf16[8,64,512]{2,1,0:T(8,128)(2,1)S(1)} collective-permute-done((bf16[8,64,512]{2,1,0:T(8,128)(2,1)S(1)}, bf16[8,64,512]{2,1,0:T(8,128)(2,1)S(1)}, u32[]{:S(2)}, u32[]{:S(2)}) %collective-permute-start.44) | collective-permute-done | bytes 524320 | tf_op jit(solution)/shard_map/ppermute | solution.py:834
  391.0 1.3 collective-permute-start.46
  393.5 1.3 collective-permute-done.46.refs_4_
  395.6 4.1 %unpack_in.1 = f32[512,2048]{1,0:T(8,128)} custom-call(s32[2]{0:T(128)} %pad_add_fusion.refs_0_, bf16[8,64,512]{2,1,0:T(8,128)(2,1)} %copy-done.14, bf16[8,64,512]{2,1,0:T(8,128)(2,1)} %copy-done.26, bf16[8,64,512]{2,1,0:T(8,128)(2,1)} %copy-done.27, bf16[8,64,512]{2,1,0:T(8,128)(2,1)} %copy-done.28, bf16[8,208,512]{2,1,0:T(8,128)(2,1)} %copy-done.3, ...), custom_call_target="tpu_custom_call" | custom-call | flops 1000000 | bytes 6291456 | tf_op jit(solution)/shard_map/unpack_in/pallas_call | solution.py:350
  (174 shorter events, 21.8 us)
Async XLA Ops:
  0.6 10.2 %collective-permute-start.1 = (bf16[512,2048]{1,0:T(8,128)(2,1)}, bf16[512,2048]{1,0:T(8,128)(2,1)S(1)}, u32[]{:S(2)}, u32[]{:S(2)}) collective-permute-start(bf16[512,2048]{1,0:T(8,128)(2,1)} %bitcast.104), channel_id=1, source_target_pairs={{0,16},{16,0},{1,17},{17,1},{2,18},{18,2},{3,19},{19,3},{4,20},{20... | collective-permute-start | bytes 6291464 | tf_op jit(solution)/shard_map/ppermute | solution.py:810
  1.2 9.7 %collective-permute-start.3 = (bf16[512,2048]{1,0:T(8,128)(2,1)}, bf16[512,2048]{1,0:T(8,128)(2,1)}, u32[]{:S(2)}, u32[]{:S(2)}) collective-permute-start(bf16[512,2048]{1,0:T(8,128)(2,1)} %bitcast.140), channel_id=1, source_target_pairs={{0,16},{16,0},{1,17},{17,1},{2,18},{18,2},{3,19},{19,3},{4,20},{20... | collective-permute-start | bytes 6291464 | tf_op jit(solution)/shard_map/ppermute | solution.py:810
  1.2 10.8 %collective-permute-start.4 = (bf16[2048,512]{1,0:T(8,128)(2,1)}, bf16[2048,512]{1,0:T(8,128)(2,1)}, u32[]{:S(2)}, u32[]{:S(2)}) collective-permute-start(bf16[2048,512]{1,0:T(8,128)(2,1)} %bitcast.144), channel_id=1, source_target_pairs={{0,16},{16,0},{1,17},{17,1},{2,18},{18,2},{3,19},{19,3},{4,20},{20... | collective-permute-start | bytes 6291464 | tf_op jit(solution)/shard_map/ppermute | solution.py:810
  3.3 7.0 %collective-permute-start = (bf16[16,512]{1,0:T(8,128)(2,1)S(1)}, bf16[16,512]{1,0:T(8,128)(2,1)S(1)}, u32[]{:S(2)}, u32[]{:S(2)}) collective-permute-start(bf16[16,512]{1,0:T(8,128)(2,1)S(1)} %concatenate.21), channel_id=1, source_target_pairs={{0,16},{16,0},{1,17},{17,1},{2,18},{18,2},{3,19},{19,3},{4,20},{20... | collective-permute-start | bytes 49160 | tf_op jit(solution)/shard_map/ppermute | solution.py:810
  3.4 7.5 %collective-permute-start.2 = (bf16[512,512]{1,0:T(8,128)(2,1)}, bf16[512,512]{1,0:T(8,128)(2,1)S(1)}, u32[]{:S(2)}, u32[]{:S(2)}) collective-permute-start(bf16[512,512]{1,0:T(8,128)(2,1)} %bitcast.149), channel_id=1, source_target_pairs={{0,16},{16,0},{1,17},{17,1},{2,18},{18,2},{3,19},{19,3},{4,20},{20... | collective-permute-start | bytes 1572872 | tf_op jit(solution)/shard_map/ppermute | solution.py:810
  99.6 18.1 %collective-permute-start.7 = (bf16[16,144,512]{2,1,0:T(8,128)(2,1)}, bf16[16,144,512]{2,1,0:T(8,128)(2,1)S(1)}, u32[]{:S(2)}, u32[]{:S(2)}) collective-permute-start(bf16[16,144,512]{2,1,0:T(8,128)(2,1)} %get-tuple-element.116), channel_id=1, source_target_pairs={{0,16},{16,0},{1,17},{17,1},{2,18},{18,2},{3,19},{19,3},{4,20},{20... | collective-permute-start | bytes 7077896 | tf_op jit(solution)/shard_map/ppermute | solution.py:810
  99.7 18.0 %copy-start.6 = (bf16[16,144,512]{2,1,0:T(8,128)(2,1)S(1)}, bf16[16,144,512]{2,1,0:T(8,128)(2,1)}, u32[]{:S(2)}) copy-start(bf16[16,144,512]{2,1,0:T(8,128)(2,1)} %get-tuple-element.109.refs_11_) | copy-start | bytes 7077892
  119.5 21.5 %collective-permute-start.8 = (bf16[8,144,512]{2,1,0:T(8,128)(2,1)S(1)}, bf16[8,144,512]{2,1,0:T(8,128)(2,1)S(1)}, u32[]{:S(2)}, u32[]{:S(2)}) collective-permute-start(bf16[8,144,512]{2,1,0:T(8,128)(2,1)S(1)} %get-tuple-element.186.refs_17_), channel_id=1, source_target_pairs={{0,1},{1,0},{2,3},{3,2},{4,5},{5,4},{6,7},{7,6},{8,9},{9,8},{10,11... | collective-permute-start | bytes 3538952 | tf_op jit(solution)/shard_map/ppermute | solution.py:834
  122.4 18.6 %copy-start.5 = (bf16[8,144,512]{2,1,0:T(8,128)(2,1)S(1)}, bf16[8,144,512]{2,1,0:T(8,128)(2,1)}, u32[]{:S(2)}) copy-start(bf16[8,144,512]{2,1,0:T(8,128)(2,1)} %get-tuple-element.185.refs_18_) | copy-start | bytes 3538948
  142.2 9.9 %collective-permute-start.9 = (bf16[4,144,512]{2,1,0:T(8,128)(2,1)S(1)}, bf16[4,144,512]{2,1,0:T(8,128)(2,1)S(1)}, u32[]{:S(2)}, u32[]{:S(2)}) collective-permute-start(bf16[4,144,512]{2,1,0:T(8,128)(2,1)S(1)} %get-tuple-element.190.refs_3_), channel_id=1, source_target_pairs={{0,2},{1,3},{2,0},{3,1},{4,6},{5,7},{6,4},{7,5},{8,10},{9,11},{10,... | collective-permute-start | bytes 1769480 | tf_op jit(solution)/shard_map/ppermute | solution.py:834
  143.7 8.4 %copy-start.12 = (bf16[4,144,512]{2,1,0:T(8,128)(2,1)S(1)}, bf16[4,144,512]{2,1,0:T(8,128)(2,1)}, u32[]{:S(2)}) copy-start(bf16[4,144,512]{2,1,0:T(8,128)(2,1)} %get-tuple-element.189.refs_4_) | copy-start | bytes 1769476
  153.0 21.1 %copy-start.23 = (bf16[16,64,512]{2,1,0:T(8,128)(2,1)S(1)}, bf16[16,64,512]{2,1,0:T(8,128)(2,1)}, u32[]{:S(2)}) copy-start(bf16[16,64,512]{2,1,0:T(8,128)(2,1)} %get-tuple-element.141) | copy-start | bytes 3145732
  174.2 10.9 %copy-start.29 = (bf16[2,144,512]{2,1,0:T(8,128)(2,1)S(1)}, bf16[2,144,512]{2,1,0:T(8,128)(2,1)}, u32[]{:S(2)}) copy-start(bf16[2,144,512]{2,1,0:T(8,128)(2,1)} %get-tuple-element.196.refs_14_) | copy-start | bytes 884740
  174.2 12.5 %copy-start.22 = (bf16[16,64,512]{2,1,0:T(8,128)(2,1)S(1)}, bf16[16,64,512]{2,1,0:T(8,128)(2,1)}, u32[]{:S(2)}) copy-start(bf16[16,64,512]{2,1,0:T(8,128)(2,1)} %get-tuple-element.128) | copy-start | bytes 3145732
  174.2 12.6 %copy-start.13 = (bf16[16,144,512]{2,1,0:T(8,128)(2,1)S(1)}, bf16[16,144,512]{2,1,0:T(8,128)(2,1)}, u32[]{:S(2)}) copy-start(bf16[16,144,512]{2,1,0:T(8,128)(2,1)} %get-tuple-element.132) | copy-start | bytes 7077892
  178.0 35.2 %collective-permute-start.11 = (bf16[16,208,512]{2,1,0:T(8,128)(2,1)}, bf16[16,208,512]{2,1,0:T(8,128)(2,1)}, u32[]{:S(2)}, u32[]{:S(2)}) collective-permute-start(bf16[16,208,512]{2,1,0:T(8,128)(2,1)} %pad_maximum_fusion), channel_id=1, source_target_pairs={{0,16},{16,0},{1,17},{17,1},{2,18},{18,2},{3,19},{19,3},{4,20},{20... | collective-permute-start | bytes 10223624 | tf_op jit(solution)/shard_map/ppermute | solution.py:810
  178.0 81.3 %collective-permute-start.5 = (f32[1024,512]{1,0:T(8,128)S(1)}, f32[1024,512]{1,0:T(8,128)}, u32[]{:S(2)}, u32[]{:S(2)}) collective-permute-start(f32[1024,512]{1,0:T(8,128)S(1)} %copy-done.1), channel_id=1, source_target_pairs={{16,0},{17,1},{18,2},{19,3},{20,4},{21,5},{22,6},{23,7},{24,8},{25... | collective-permute-start | bytes 6291464 | tf_op jit(solution)/shard_map/ppermute | solution.py:814
  179.3 78.4 %collective-permute-start.6 = (f32[1024,512]{1,0:T(8,128)}, f32[1024,512]{1,0:T(8,128)}, u32[]{:S(2)}, u32[]{:S(2)}) collective-permute-start(f32[1024,512]{1,0:T(8,128)} %get-tuple-element.98.refs_3_), channel_id=1, source_target_pairs={{0,16},{1,17},{2,18},{3,19},{4,20},{5,21},{6,22},{7,23},{8,24},{9,... | collective-permute-start | bytes 6291464 | tf_op jit(solution)/shard_map/ppermute | solution.py:814
  185.1 6.7 %collective-permute-start.10 = (bf16[2,144,512]{2,1,0:T(8,128)(2,1)S(1)}, bf16[2,144,512]{2,1,0:T(8,128)(2,1)S(1)}, u32[]{:S(2)}, u32[]{:S(2)}) collective-permute-start(bf16[2,144,512]{2,1,0:T(8,128)(2,1)S(1)} %copy-done.29), channel_id=1, source_target_pairs={{0,4},{1,5},{2,6},{3,7},{4,0},{5,1},{6,2},{7,3},{8,12},{9,13},{10,... | collective-permute-start | bytes 884744 | tf_op jit(solution)/shard_map/ppermute | solution.py:834
  186.9 8.2 %copy-start.2 = (bf16[16,208,512]{2,1,0:T(8,128)(2,1)}, bf16[16,208,512]{2,1,0:T(8,128)(2,1)S(1)}, u32[]{:S(2)}) copy-start(bf16[16,208,512]{2,1,0:T(8,128)(2,1)S(1)} %constant_dynamic-update-slice_fusion.refs_11_) | copy-start | bytes 10223620
  192.6 27.0 %collective-permute-start.12 = (bf16[144,512]{1,0:T(8,128)(2,1)S(1)}, bf16[144,512]{1,0:T(8,128)(2,1)S(1)}, u32[]{:S(2)}, u32[]{:S(2)}) collective-permute-start(bf16[144,512]{1,0:T(8,128)(2,1)S(1)} %get-tuple-element.202.refs_12_), channel_id=1, source_target_pairs={{0,8},{4,12},{8,0},{12,4},{1,9},{5,13},{9,1},{13,5},{2,10},{6,14},... | collective-permute-start | bytes 442376 | tf_op jit(solution)/shard_map/ppermute | solution.py:818
  218.5 35.9 %collective-permute-start.16 = (bf16[8,208,512]{2,1,0:T(8,128)(2,1)S(1)}, bf16[8,208,512]{2,1,0:T(8,128)(2,1)}, u32[]{:S(2)}, u32[]{:S(2)}) collective-permute-start(bf16[8,208,512]{2,1,0:T(8,128)(2,1)S(1)} %get-tuple-element.184.refs_17_), channel_id=1, source_target_pairs={{0,1},{1,0},{2,3},{3,2},{4,5},{5,4},{6,7},{7,6},{8,9},{9,8},{10,11... | collective-permute-start | bytes 5111816 | tf_op jit(solution)/shard_map/ppermute | solution.py:834
  220.3 19.8 %copy-start.15 = (bf16[144,512]{1,0:T(8,128)(2,1)S(1)}, bf16[144,512]{1,0:T(8,128)(2,1)}, u32[]{:S(2)}) copy-start(bf16[144,512]{1,0:T(8,128)(2,1)} %add_convert_fusion.17.refs_19_) | copy-start | bytes 442372
  238.8 29.1 %collective-permute-start.13 = (f32[1024,512]{1,0:T(8,128)}, f32[1024,512]{1,0:T(8,128)}, u32[]{:S(2)}, u32[]{:S(2)}) collective-permute-start(f32[1024,512]{1,0:T(8,128)} %get-tuple-element.145.refs_1_), channel_id=1, source_target_pairs={{16,0},{17,1},{18,2},{19,3},{20,4},{21,5},{22,6},{23,7},{24,8},{25... | collective-permute-start | bytes 6291464 | tf_op jit(solution)/shard_map/ppermute | solution.py:814
  240.1 9.7 %collective-permute-start.18 = (bf16[144,512]{1,0:T(8,128)(2,1)S(1)}, bf16[144,512]{1,0:T(8,128)(2,1)S(1)}, u32[]{:S(2)}, u32[]{:S(2)}) collective-permute-start(bf16[144,512]{1,0:T(8,128)(2,1)S(1)} %copy-done.15), channel_id=1, source_target_pairs={{0,8},{4,12},{8,0},{12,4},{1,9},{5,13},{9,1},{13,5},{2,10},{6,14},... | collective-permute-start | bytes 442376 | tf_op jit(solution)/shard_map/ppermute | solution.py:818
  240.8 14.1 %copy-start.4 = (bf16[8,208,512]{2,1,0:T(8,128)(2,1)S(1)}, bf16[8,208,512]{2,1,0:T(8,128)(2,1)}, u32[]{:S(2)}) copy-start(bf16[8,208,512]{2,1,0:T(8,128)(2,1)} %get-tuple-element.183.refs_18_) | copy-start | bytes 5111812
  249.7 18.1 %collective-permute-start.14 = (bf16[1024,512]{1,0:T(8,128)(2,1)}, bf16[1024,512]{1,0:T(8,128)(2,1)}, u32[]{:S(2)}, u32[]{:S(2)}) collective-permute-start(bf16[1024,512]{1,0:T(8,128)(2,1)} %get-tuple-element.118.refs_1_.refs_3_), channel_id=1, source_target_pairs={{0,16},{1,17},{2,18},{3,19},{4,20},{5,21},{6,22},{7,23},{8,24},{9,... | collective-permute-start | bytes 3145736 | tf_op jit(solution)/shard_map/ppermute | solution.py:814
  254.4 11.7 %collective-permute-start.19 = (bf16[2,144,512]{2,1,0:T(8,128)(2,1)}, bf16[2,144,512]{2,1,0:T(8,128)(2,1)}, u32[]{:S(2)}, u32[]{:S(2)}) collective-permute-start(bf16[2,144,512]{2,1,0:T(8,128)(2,1)} %get-tuple-element.208), channel_id=1, source_target_pairs={{0,4},{1,5},{2,6},{3,7},{4,0},{5,1},{6,2},{7,3},{8,12},{9,13},{10,... | collective-permute-start | bytes 884744 | tf_op jit(solution)/shard_map/ppermute | solution.py:834
  257.7 16.3 %collective-permute-start.17 = (bf16[4,208,512]{2,1,0:T(8,128)(2,1)}, bf16[4,208,512]{2,1,0:T(8,128)(2,1)S(1)}, u32[]{:S(2)}, u32[]{:S(2)}) collective-permute-start(bf16[4,208,512]{2,1,0:T(8,128)(2,1)} %get-tuple-element.188), channel_id=1, source_target_pairs={{0,2},{1,3},{2,0},{3,1},{4,6},{5,7},{6,4},{7,5},{8,10},{9,11},{10,... | collective-permute-start | bytes 2555912 | tf_op jit(solution)/shard_map/ppermute | solution.py:834
  259.3 6.8 %copy-start.30 = (f32[16,512]{1,0:T(8,128)S(1)}, f32[16,512]{1,0:T(8,128)}, u32[]{:S(2)}) copy-start(f32[16,512]{1,0:T(8,128)} %get-tuple-element.147) | copy-start | bytes 98308
  259.3 6.8 %copy-start.31 = (f32[16,512]{1,0:T(8,128)S(1)}, f32[16,512]{1,0:T(8,128)}, u32[]{:S(2)}) copy-start(f32[16,512]{1,0:T(8,128)} %get-tuple-element.124) | copy-start | bytes 98308
  266.0 12.3 %collective-permute-start.21 = (bf16[16,64,512]{2,1,0:T(8,128)(2,1)}, bf16[16,64,512]{2,1,0:T(8,128)(2,1)S(1)}, u32[]{:S(2)}, u32[]{:S(2)}) collective-permute-start(bf16[16,64,512]{2,1,0:T(8,128)(2,1)} %get-tuple-element.158), channel_id=1, source_target_pairs={{0,16},{16,0},{1,17},{17,1},{2,18},{18,2},{3,19},{19,3},{4,20},{20... | collective-permute-start | bytes 3145736 | tf_op jit(solution)/shard_map/ppermute | solution.py:810
  267.2 9.9 %collective-permute-start.23 = (bf16[4,144,512]{2,1,0:T(8,128)(2,1)S(1)}, bf16[4,144,512]{2,1,0:T(8,128)(2,1)S(1)}, u32[]{:S(2)}, u32[]{:S(2)}) collective-permute-start(bf16[4,144,512]{2,1,0:T(8,128)(2,1)S(1)} %bitcast.118), channel_id=1, source_target_pairs={{0,2},{1,3},{2,0},{3,1},{4,6},{5,7},{6,4},{7,5},{8,10},{9,11},{10,... | collective-permute-start | bytes 1769480 | tf_op jit(solution)/shard_map/ppermute | solution.py:834
  274.2 8.2 %collective-permute-start.22 = (bf16[2,208,512]{2,1,0:T(8,128)(2,1)S(1)}, bf16[2,208,512]{2,1,0:T(8,128)(2,1)S(1)}, u32[]{:S(2)}, u32[]{:S(2)}) collective-permute-start(bf16[2,208,512]{2,1,0:T(8,128)(2,1)S(1)} %get-tuple-element.194), channel_id=1, source_target_pairs={{0,4},{1,5},{2,6},{3,7},{4,0},{5,1},{6,2},{7,3},{8,12},{9,13},{10,... | collective-permute-start | bytes 1277960 | tf_op jit(solution)/shard_map/ppermute | solution.py:834
  277.3 79.9 %copy-start.11 = (bf16[8,144,512]{2,1,0:T(8,128)(2,1)}, bf16[8,144,512]{2,1,0:T(8,128)(2,1)S(1)}, u32[]{:S(2)}) copy-start(bf16[8,144,512]{2,1,0:T(8,128)(2,1)S(1)} %pad_maximum_fusion.2.refs_5_) | copy-start | bytes 3538948
  277.3 26.8 %collective-permute-start.27 = (bf16[8,144,512]{2,1,0:T(8,128)(2,1)S(1)}, bf16[8,144,512]{2,1,0:T(8,128)(2,1)S(1)}, u32[]{:S(2)}, u32[]{:S(2)}) collective-permute-start(bf16[8,144,512]{2,1,0:T(8,128)(2,1)S(1)} %pad_maximum_fusion.2.refs_5_), channel_id=1, source_target_pairs={{0,1},{1,0},{2,3},{3,2},{4,5},{5,4},{6,7},{7,6},{8,9},{9,8},{10,11... | collective-permute-start | bytes 3538952 | tf_op jit(solution)/shard_map/ppermute | solution.py:834
  278.6 23.0 %collective-permute-start.25 = (bf16[8,64,512]{2,1,0:T(8,128)(2,1)S(1)}, bf16[8,64,512]{2,1,0:T(8,128)(2,1)S(1)}, u32[]{:S(2)}, u32[]{:S(2)}) collective-permute-start(bf16[8,64,512]{2,1,0:T(8,128)(2,1)S(1)} %get-tuple-element.192), channel_id=1, source_target_pairs={{0,1},{1,0},{2,3},{3,2},{4,5},{5,4},{6,7},{7,6},{8,9},{9,8},{10,11... | collective-permute-start | bytes 1572872 | tf_op jit(solution)/shard_map/ppermute | solution.py:834
  282.5 19.1 %collective-permute-start.26 = (bf16[208,512]{1,0:T(8,128)(2,1)S(1)}, bf16[208,512]{1,0:T(8,128)(2,1)S(1)}, u32[]{:S(2)}, u32[]{:S(2)}) collective-permute-start(bf16[208,512]{1,0:T(8,128)(2,1)S(1)} %get-tuple-element.200), channel_id=1, source_target_pairs={{0,8},{4,12},{8,0},{12,4},{1,9},{5,13},{9,1},{13,5},{2,10},{6,14},... | collective-permute-start | bytes 638984 | tf_op jit(solution)/shard_map/ppermute | solution.py:818
  284.8 1.2 collective-permute-start.15
  286.1 15.5 %collective-permute-start.20 = (f32[24,512]{1,0:T(8,128)S(1)}, f32[24,512]{1,0:T(8,128)S(1)}, u32[]{:S(2)}, u32[]{:S(2)}) collective-permute-start(f32[24,512]{1,0:T(8,128)S(1)} %add.144), channel_id=1, source_target_pairs={{0,1},{1,0},{2,3},{3,2},{4,5},{5,4},{6,7},{7,6},{8,9},{9,8},{10,11... | collective-permute-start | bytes 147464 | tf_op jit(solution)/shard_map/ppermute | solution.py:818
  301.7 9.2 %collective-permute-start.30 = (bf16[208,512]{1,0:T(8,128)(2,1)S(1)}, bf16[208,512]{1,0:T(8,128)(2,1)S(1)}, u32[]{:S(2)}, u32[]{:S(2)}) collective-permute-start(bf16[208,512]{1,0:T(8,128)(2,1)S(1)} %add_convert_fusion.16), channel_id=1, source_target_pairs={{0,8},{4,12},{8,0},{12,4},{1,9},{5,13},{9,1},{13,5},{2,10},{6,14},... | collective-permute-start | bytes 638984 | tf_op jit(solution)/shard_map/ppermute | solution.py:818
  303.0 9.4 %collective-permute-start.29 = (bf16[4,64,512]{2,1,0:T(8,128)(2,1)S(1)}, bf16[4,64,512]{2,1,0:T(8,128)(2,1)S(1)}, u32[]{:S(2)}, u32[]{:S(2)}) collective-permute-start(bf16[4,64,512]{2,1,0:T(8,128)(2,1)S(1)} %get-tuple-element.198), channel_id=1, source_target_pairs={{0,2},{1,3},{2,0},{3,1},{4,6},{5,7},{6,4},{7,5},{8,10},{9,11},{10,... | collective-permute-start | bytes 786440 | tf_op jit(solution)/shard_map/ppermute | solution.py:834
  304.1 55.5 %copy-start.17 = (bf16[8,144,512]{2,1,0:T(8,128)(2,1)}, bf16[8,144,512]{2,1,0:T(8,128)(2,1)S(1)}, u32[]{:S(2)}) copy-start(bf16[8,144,512]{2,1,0:T(8,128)(2,1)S(1)} %collective-permute-done.27.refs_6_) | copy-start | bytes 3538948
  310.9 10.8 %collective-permute-start.33 = (bf16[2,208,512]{2,1,0:T(8,128)(2,1)S(1)}, bf16[2,208,512]{2,1,0:T(8,128)(2,1)S(1)}, u32[]{:S(2)}, u32[]{:S(2)}) collective-permute-start(bf16[2,208,512]{2,1,0:T(8,128)(2,1)S(1)} %get-tuple-element.206), channel_id=1, source_target_pairs={{0,4},{1,5},{2,6},{3,7},{4,0},{5,1},{6,2},{7,3},{8,12},{9,13},{10,... | collective-permute-start | bytes 1277960 | tf_op jit(solution)/shard_map/ppermute | solution.py:834
  311.0 4.2 %collective-permute-start.24 = (f32[24,512]{1,0:T(8,128)S(1)}, f32[24,512]{1,0:T(8,128)S(1)}, u32[]{:S(2)}, u32[]{:S(2)}) collective-permute-start(f32[24,512]{1,0:T(8,128)S(1)} %add.149), channel_id=1, source_target_pairs={{0,2},{1,3},{2,0},{3,1},{4,6},{5,7},{6,4},{7,5},{8,10},{9,11},{10,... | collective-permute-start | bytes 147464 | tf_op jit(solution)/shard_map/ppermute | solution.py:818
  321.8 13.3 %collective-permute-start.36 = (bf16[4,208,512]{2,1,0:T(8,128)(2,1)S(1)}, bf16[4,208,512]{2,1,0:T(8,128)(2,1)S(1)}, u32[]{:S(2)}, u32[]{:S(2)}) collective-permute-start(bf16[4,208,512]{2,1,0:T(8,128)(2,1)S(1)} %bitcast.115), channel_id=1, source_target_pairs={{0,2},{1,3},{2,0},{3,1},{4,6},{5,7},{6,4},{7,5},{8,10},{9,11},{10,... | collective-permute-start | bytes 2555912 | tf_op jit(solution)/shard_map/ppermute | solution.py:834
  321.9 7.6 %collective-permute-start.32 = (bf16[2,64,512]{2,1,0:T(8,128)(2,1)S(1)}, bf16[2,64,512]{2,1,0:T(8,128)(2,1)S(1)}, u32[]{:S(2)}, u32[]{:S(2)}) collective-permute-start(bf16[2,64,512]{2,1,0:T(8,128)(2,1)S(1)} %get-tuple-element.204), channel_id=1, source_target_pairs={{0,4},{1,5},{2,6},{3,7},{4,0},{5,1},{6,2},{7,3},{8,12},{9,13},{10,... | collective-permute-start | bytes 393224 | tf_op jit(solution)/shard_map/ppermute | solution.py:834
  322.0 7.5 %collective-permute-start.28 = (f32[24,512]{1,0:T(8,128)S(1)}, f32[24,512]{1,0:T(8,128)S(1)}, u32[]{:S(2)}, u32[]{:S(2)}) collective-permute-start(f32[24,512]{1,0:T(8,128)S(1)} %add.153), channel_id=1, source_target_pairs={{0,4},{4,0},{8,12},{12,8},{1,5},{5,1},{9,13},{13,9},{2,6},{6,2},{1... | collective-permute-start | bytes 147464 | tf_op jit(solution)/shard_map/ppermute | solution.py:818
  335.2 32.5 %copy-start.3 = (bf16[8,208,512]{2,1,0:T(8,128)(2,1)}, bf16[8,208,512]{2,1,0:T(8,128)(2,1)S(1)}, u32[]{:S(2)}) copy-start(bf16[8,208,512]{2,1,0:T(8,128)(2,1)S(1)} %pad_maximum_fusion.1.refs_1_.refs_5_) | copy-start | bytes 5111812
  335.3 21.9 %collective-permute-start.38 = (bf16[8,208,512]{2,1,0:T(8,128)(2,1)S(1)}, bf16[8,208,512]{2,1,0:T(8,128)(2,1)S(1)}, u32[]{:S(2)}, u32[]{:S(2)}) collective-permute-start(bf16[8,208,512]{2,1,0:T(8,128)(2,1)S(1)} %pad_maximum_fusion.1.refs_1_.refs_5_), channel_id=1, source_target_pairs={{0,1},{1,0},{2,3},{3,2},{4,5},{5,4},{6,7},{7,6},{8,9},{9,8},{10,11... | collective-permute-start | bytes 5111816 | tf_op jit(solution)/shard_map/ppermute | solution.py:834
  336.3 5.2 %collective-permute-start.34 = (bf16[64,512]{1,0:T(8,128)(2,1)S(1)}, bf16[64,512]{1,0:T(8,128)(2,1)S(1)}, u32[]{:S(2)}, u32[]{:S(2)}) collective-permute-start(bf16[64,512]{1,0:T(8,128)(2,1)S(1)} %get-tuple-element.210), channel_id=1, source_target_pairs={{0,8},{4,12},{8,0},{12,4},{1,9},{5,13},{9,1},{13,5},{2,10},{6,14},... | collective-permute-start | bytes 196616 | tf_op jit(solution)/shard_map/ppermute | solution.py:818
  336.3 5.7 %collective-permute-start.31 = (f32[24,512]{1,0:T(8,128)S(1)}, f32[24,512]{1,0:T(8,128)S(1)}, u32[]{:S(2)}, u32[]{:S(2)}) collective-permute-start(f32[24,512]{1,0:T(8,128)S(1)} %add.156), channel_id=1, source_target_pairs={{0,8},{4,12},{8,0},{12,4},{1,9},{5,13},{9,1},{13,5},{2,10},{6,14},... | collective-permute-start | bytes 147464 | tf_op jit(solution)/shard_map/ppermute | solution.py:818
  342.0 24.4 %collective-permute-start.39 = (bf16[8,208,512]{2,1,0:T(8,128)(2,1)S(1)}, bf16[8,208,512]{2,1,0:T(8,128)(2,1)S(1)}, u32[]{:S(2)}, u32[]{:S(2)}) collective-permute-start(bf16[8,208,512]{2,1,0:T(8,128)(2,1)S(1)} %pad_maximum_fusion.1.refs_1_.refs_5_), channel_id=1, source_target_pairs={{0,16},{16,0},{1,17},{17,1},{2,18},{18,2},{3,19},{19,3},{4,20},{20... | collective-permute-start | bytes 5111816 | tf_op jit(solution)/shard_map/ppermute | solution.py:810
  357.1 10.6 %copy-start.7 = (bf16[8,208,512]{2,1,0:T(8,128)(2,1)}, bf16[8,208,512]{2,1,0:T(8,128)(2,1)S(1)}, u32[]{:S(2)}) copy-start(bf16[8,208,512]{2,1,0:T(8,128)(2,1)S(1)} %collective-permute-done.38.refs_2_.refs_6_) | copy-start | bytes 5111812
  357.1 10.6 %collective-permute-start.40 = (bf16[8,208,512]{2,1,0:T(8,128)(2,1)S(1)}, bf16[8,208,512]{2,1,0:T(8,128)(2,1)}, u32[]{:S(2)}, u32[]{:S(2)}) collective-permute-start(bf16[8,208,512]{2,1,0:T(8,128)(2,1)S(1)} %collective-permute-done.38.refs_2_.refs_6_), channel_id=1, source_target_pairs={{0,16},{16,0},{1,17},{17,1},{2,18},{18,2},{3,19},{19,3},{4,20},{20... | collective-permute-start | bytes 5111816 | tf_op jit(solution)/shard_map/ppermute | solution.py:810
  357.2 9.2 %collective-permute-start.41 = (bf16[8,144,512]{2,1,0:T(8,128)(2,1)S(1)}, bf16[8,144,512]{2,1,0:T(8,128)(2,1)S(1)}, u32[]{:S(2)}, u32[]{:S(2)}) collective-permute-start(bf16[8,144,512]{2,1,0:T(8,128)(2,1)S(1)} %pad_maximum_fusion.2.refs_5_), channel_id=1, source_target_pairs={{0,16},{1,17},{2,18},{3,19},{4,20},{5,21},{6,22},{7,23},{8,24},{9,... | collective-permute-start | bytes 3538952 | tf_op jit(solution)/shard_map/ppermute | solution.py:814
  359.6 6.7 %collective-permute-start.42 = (bf16[8,144,512]{2,1,0:T(8,128)(2,1)S(1)}, bf16[8,144,512]{2,1,0:T(8,128)(2,1)S(1)}, u32[]{:S(2)}, u32[]{:S(2)}) collective-permute-start(bf16[8,144,512]{2,1,0:T(8,128)(2,1)S(1)} %collective-permute-done.27.refs_6_), channel_id=1, source_target_pairs={{0,16},{1,17},{2,18},{3,19},{4,20},{5,21},{6,22},{7,23},{8,24},{9,... | collective-permute-start | bytes 3538952 | tf_op jit(solution)/shard_map/ppermute | solution.py:814
  361.0 5.2 %collective-permute-start.35 = (bf16[64,512]{1,0:T(8,128)(2,1)S(1)}, bf16[64,512]{1,0:T(8,128)(2,1)S(1)}, u32[]{:S(2)}, u32[]{:S(2)}) collective-permute-start(bf16[64,512]{1,0:T(8,128)(2,1)S(1)} %add_convert_fusion.20), channel_id=1, source_target_pairs={{0,8},{4,12},{8,0},{12,4},{1,9},{5,13},{9,1},{13,5},{2,10},{6,14},... | collective-permute-start | bytes 196616 | tf_op jit(solution)/shard_map/ppermute | solution.py:818
  366.3 8.9 %collective-permute-start.37 = (bf16[2,64,512]{2,1,0:T(8,128)(2,1)S(1)}, bf16[2,64,512]{2,1,0:T(8,128)(2,1)S(1)}, u32[]{:S(2)}, u32[]{:S(2)}) collective-permute-start(bf16[2,64,512]{2,1,0:T(8,128)(2,1)S(1)} %get-tuple-element.212), channel_id=1, source_target_pairs={{0,4},{1,5},{2,6},{3,7},{4,0},{5,1},{6,2},{7,3},{8,12},{9,13},{10,... | collective-permute-start | bytes 393224 | tf_op jit(solution)/shard_map/ppermute | solution.py:834
  375.2 6.4 %collective-permute-start.43 = (bf16[4,64,512]{2,1,0:T(8,128)(2,1)S(1)}, bf16[4,64,512]{2,1,0:T(8,128)(2,1)S(1)}, u32[]{:S(2)}, u32[]{:S(2)}) collective-permute-start(bf16[4,64,512]{2,1,0:T(8,128)(2,1)S(1)} %bitcast.123), channel_id=1, source_target_pairs={{0,2},{1,3},{2,0},{3,1},{4,6},{5,7},{6,4},{7,5},{8,10},{9,11},{10,... | collective-permute-start | bytes 786440 | tf_op jit(solution)/shard_map/ppermute | solution.py:834
  381.7 13.1 %copy-start.14 = (bf16[8,64,512]{2,1,0:T(8,128)(2,1)}, bf16[8,64,512]{2,1,0:T(8,128)(2,1)S(1)}, u32[]{:S(2)}) copy-start(bf16[8,64,512]{2,1,0:T(8,128)(2,1)S(1)} %pad_maximum_fusion.5.refs_1_) | copy-start | bytes 1572868
  381.7 9.2 %collective-permute-start.44 = (bf16[8,64,512]{2,1,0:T(8,128)(2,1)S(1)}, bf16[8,64,512]{2,1,0:T(8,128)(2,1)S(1)}, u32[]{:S(2)}, u32[]{:S(2)}) collective-permute-start(bf16[8,64,512]{2,1,0:T(8,128)(2,1)S(1)} %pad_maximum_fusion.5.refs_1_), channel_id=1, source_target_pairs={{0,1},{1,0},{2,3},{3,2},{4,5},{5,4},{6,7},{7,6},{8,9},{9,8},{10,11... | collective-permute-start | bytes 1572872 | tf_op jit(solution)/shard_map/ppermute | solution.py:834
  384.0 9.5 %collective-permute-start.45 = (bf16[8,64,512]{2,1,0:T(8,128)(2,1)S(1)}, bf16[8,64,512]{2,1,0:T(8,128)(2,1)S(1)}, u32[]{:S(2)}, u32[]{:S(2)}) collective-permute-start(bf16[8,64,512]{2,1,0:T(8,128)(2,1)S(1)} %pad_maximum_fusion.5.refs_1_), channel_id=1, source_target_pairs={{16,0},{17,1},{18,2},{19,3},{20,4},{21,5},{22,6},{23,7},{24,8},{25... | collective-permute-start | bytes 1572872 | tf_op jit(solution)/shard_map/ppermute | solution.py:814
  391.0 3.8 collective-permute-start.46
  (20 other events, 53.8 us)

commit v2 on v1

--- a/solution.py
+++ b/solution.py
@@ -18,7 +18,7 @@
 ROWS = 256
 STEPS = LEN // ROWS
 SUBS = ROWS // C
-BACK_STEPS = 2
+BACK_STEPS = 4
 EPSILON = 1e-05
 F32 = jnp.float32
 BF16 = jnp.bfloat16

time: 408 us -> 407 us (level)
  starting transfers between devices: 51.8 us -> 77.1 us
  waiting for transfers between devices: 92.8 us -> 77.6 us
  Pallas kernels: 218 us -> 209 us
    ppermute x10, starting transfers between devices: 1.9 us -> 24.1 us  [cores_swap(): return lax.ppermute(x, 'section', [(0, 1), (1, 0)])]
    ppermute x11, waiting for transfers between devices: 40.7 us -> 29.2 us  [exchange(): lax.ppermute(x, axis, [(i, i ^ by) for i in range(lax.axis_size(axis))])]
    pallas_call x13 -> x11, Pallas kernels: 218 us -> 209 us  [call(): pl.pallas_call(body, grid_spec=pltpu.PrefetchScalarGridSpec(num_scalar_pr...]
    ppermute x18, starting transfers between devices: 16.9 us -> 22.5 us  [exchange_by_core(): return lax.ppermute(x, ('section', 'dp', 'rep'), pairs)]
  transfers between devices with their start and end apart: 47 -> 47, of which waited for: 20 -> 23; matrix products, arithmetic and copies ran while one was open for 6% -> 5% of each run, Pallas kernels for 26% -> 24%
where the time goes in v2:
time: 407 us; the launch traced here: 401 us
  Pallas kernels  209 us (51%)
  waiting for transfers between devices  77.6 us (19%)
  starting transfers between devices  77.1 us (19%)
  other arithmetic  23.8 us (6%)
  local copies, waits for them, and re-layouts  9.89 us (2%)
    pallas_call x11, Pallas kernels, call(): pl.pallas_call(body, grid_spec=pltpu.PrefetchScalarGridSpec(num_scalar_pr...  209 us
    ppermute x18, waiting for transfers between devices, exchange_by_core(): return lax.ppermute(x, ('section', 'dp', 'rep'), pairs)  46 us
    ppermute x11, waiting for transfers between devices, exchange(): lax.ppermute(x, axis, [(i, i ^ by) for i in range(lax.axis_size(axis))])  29.2 us
    ppermute x10, starting transfers between devices, cores_swap(): return lax.ppermute(x, 'section', [(0, 1), (1, 0)])  24.1 us
    ppermute x18, starting transfers between devices, exchange_by_core(): return lax.ppermute(x, ('section', 'dp', 'rep'), pairs)  22.5 us
    ppermute x8, starting transfers between devices, to_core(): return lax.ppermute(x, 'section', [(1 - core, core)])  17 us
    convert_element_type x15, other arithmetic, add_low(): return total.astype(BF16)  13.5 us
    ppermute x11, starting transfers between devices, exchange(): lax.ppermute(x, axis, [(i, i ^ by) for i in range(lax.axis_size(axis))])  13.5 us
  transfers between devices with their start and end apart: 47, of which 23 were waited for; matrix products, arithmetic and copies ran while one was open for 5% of the time, Pallas kernels for 24%

profile of v2, /device:TPU:0, one launch (start us, length us, event | category | flops | bytes accessed | tf_op | source)
XLA Modules:
  0.0 400.5 jit_solution(3548942523909776508)
XLA Ops:
  3.8 1.3 fusion.21
  6.5 1.3 fusion.16
  7.8 1.9 fusion.17
  12.4 36.7 %forward0.1 = (f32[1024,512]{1,0:T(8,128)}, bf16[1024,512]{1,0:T(8,128)(2,1)}, bf16[1024,2048]{1,0:T(8,128)(2,1)}, f32[3,1024,512]{2,1,0:T(8,128)}, bf16[8,4,128...) custom-call(s32[2]{0:T(128)} %pad_add_fusion.refs_0_, ...), custom_call_target="tpu_custom_call" | custom-call | flops 15000000512 | bytes 33000000 | tf_op jit(solution)/shard_map/forward0/pallas_call | solution.py:350
  49.1 50.4 %forward1.1 = (f32[1024,512]{1,0:T(8,128)}, bf16[1024,512]{1,0:T(8,128)(2,1)}, bf16[1024,2048]{1,0:T(8,128)(2,1)}, f32[3,1024,512]{2,1,0:T(8,128)}, bf16[8,4,128...) custom-call(s32[2]{0:T(128)} %pad_add_fusion.refs_0_, ...), custom_call_target="tpu_custom_call" | custom-call | flops 24999999488 | bytes 33000000 | tf_op jit(solution)/shard_map/forward1/pallas_call | solution.py:350
  99.7 32.1 %backward_attention1.1 = (bf16[1024,512]{1,0:T(8,128)(2,1)}, bf16[1024,2048]{1,0:T(8,128)(2,1)}, f32[4,128,128]{2,1,0:T(8,128)}, f32[4,128,128]{2,1,0:T(8,128)}, f32[1,512]{1,0:T(1,128)}, /*index=5*/f32[16,512]{1,0:T(8,128)}) custom-call(s32[2]{0:T(128)} %pad_add_fusion.refs_0_, f32[1024,512]{1,0:T(8,128)} %get-tuple-element.85.refs_2_.refs_1_, ...), custom_call_target="tpu_custom_call" | custom-call | flops 8999999488 | bytes 17000000 | tf_op jit(solution)/shard_map/backward_attention1/pallas_call | solution.py:350
  131.8 1.8 add_convert_fusion.2
  133.5 2.9 collective-permute-start.8
  136.5 6.7 %in_grad.2 = (bf16[16,64,512]{2,1,0:T(8,128)(2,1)}, bf16[16,64,512]{2,1,0:T(8,128)(2,1)}) custom-call(s32[2]{0:T(128)} %pad_add_fusion.refs_0_, bf16[1024,512]{1,0:T(8,128)(2,1)} %get-tuple-element.107.refs_1_, bf16[1024,2048]{1,0:T(8,128)(2,1)} %get-tuple-element.108.refs_2_, bf16[8,144,512]{2,1,0:T(8,128)(2,1)} %copy-done.15, ...), custom_call_target="tpu_custom_call" | custom-call | flops 2200000000 | bytes 7000000 | tf_op jit(solution)/shard_map/in_grad/pallas_call | solution.py:350
  143.2 7.5 %collective-permute-done.8 = bf16[8,144,512]{2,1,0:T(8,128)(2,1)S(1)} collective-permute-done((bf16[8,144,512]{2,1,0:T(8,128)(2,1)S(1)}, bf16[8,144,512]{2,1,0:T(8,128)(2,1)S(1)}, u32[]{:S(2)}, u32[]{:S(2)}) %collective-permute-start.8) | collective-permute-done | bytes 1179680 | tf_op jit(solution)/shard_map/ppermute | solution.py:834
  150.6 1.4 add_convert_fusion.6
  152.0 21.3 %backward_ffn0.1 = (f32[1024,512]{1,0:T(8,128)}, bf16[1024,512]{1,0:T(8,128)(2,1)}, f32[16,512]{1,0:T(8,128)}, bf16[16,144,512]{2,1,0:T(8,128)(2,1)}, bf16[16,144,512]{2,1,0:T(8,128)(2,1)}) custom-call(s32[2]{0:T(128)} %pad_add_fusion.refs_0_, bf16[1024,512]{1,0:T(8,128)(2,1)} %get-tuple-element.98.refs_1_.refs_3_, f32[1024,512]{1,0:T(8,128)} %get-tuple-element.99.refs_2_, ...), custom_call_target="tpu_custom_call" | custom-call | flops 12000000000 | bytes 27000000 | tf_op jit(solution)/shard_map/backward_ffn0/pallas_call | solution.py:350
  173.4 3.8 pad_maximum_fusion
  177.2 2.1 collective-permute-start.9
  179.3 1.3 collective-permute-start.5
  180.6 5.7 %collective-permute-start.6 = (f32[1024,512]{1,0:T(8,128)}, f32[1024,512]{1,0:T(8,128)}, u32[]{:S(2)}, u32[]{:S(2)}) collective-permute-start(f32[1024,512]{1,0:T(8,128)} %get-tuple-element.86.refs_3_), channel_id=1, source_target_pairs={{0,16},{1,17},{2,18},{3,19},{4,20},{5,21},{6,22},{7,23},{8,24},{9,... | collective-permute-start | bytes 6291464 | tf_op jit(solution)/shard_map/ppermute | solution.py:814
  188.5 32.2 %backward_attention0.1 = (f32[1024,512]{1,0:T(8,128)}, bf16[1024,2048]{1,0:T(8,128)(2,1)}, f32[4,128,128]{2,1,0:T(8,128)}, f32[4,128,128]{2,1,0:T(8,128)}, f32[1,512]{1,0:T(1,128)}, /*index=5*/f32[16,512]{1,0:T(8,128)}) custom-call(s32[2]{0:T(128)} %pad_add_fusion.refs_0_, bf16[2048,512]{1,0:T(8,128)(2,1)} %refs_1_.3, ...), custom_call_target="tpu_custom_call" | custom-call | flops 8999999488 | bytes 17000000 | tf_op jit(solution)/shard_map/backward_attention0/pallas_call | solution.py:350
  220.7 6.9 %in_grad.3 = (bf16[16,64,512]{2,1,0:T(8,128)(2,1)}, bf16[16,64,512]{2,1,0:T(8,128)(2,1)}) custom-call(s32[2]{0:T(128)} %pad_add_fusion.refs_0_, bf16[1024,512]{1,0:T(8,128)(2,1)} %get-tuple-element.121.refs_1_, bf16[1024,2048]{1,0:T(8,128)(2,1)} %get-tuple-element.122.refs_2_), custom_call_target="tpu_custom_call" | custom-call | flops 2200000000 | bytes 7000000 | tf_op jit(solution)/shard_map/in_grad/pallas_call | solution.py:350
  227.7 4.2 %add_convert_fusion = (bf16[8,208,512]{2,1,0:T(8,128)(2,1)}, bf16[8,208,512]{2,1,0:T(8,128)(2,1)S(1)}) fusion(bf16[16,208,512]{2,1,0:T(8,128)(2,1)S(1)} %copy-done.4, bf16[16,208,512]{2,1,0:T(8,128)(2,1)} %collective-permute-done.13), kind=kLoop, calls=%fused_computation.1 | loop fusion | flops 6815744 | bytes 10223616 | tf_op jit(solution)/shard_map/convert_element_type | solution.py:825
  232.0 1.6 collective-permute-start.14
  233.6 1.3 collective-permute-start.10
  234.9 1.7 collective-permute-start.15
  236.7 2.8 collective-permute-start.11
  239.6 6.6 %layer_outputs.1 = f32[2048,512]{1,0:T(8,128)} custom-call(s32[2]{0:T(128)} %pad_add_fusion.refs_0_, f32[1024,512]{1,0:T(8,128)} %get-tuple-element.85.refs_2_.refs_1_, f32[1024,512]{1,0:T(8,128)} %collective-permute-done.5.refs_2_, f32[1024,512]{1,0:T(8,128)} %get-tuple-element.86.refs_3_, f32[1024,512]{1,0:T(8,128)} %collective-permute-done.6.refs_4_), custom_call_target="tpu_custom_call" | custom-call | flops 1000000 | bytes 8000000 | tf_op jit(solution)/shard_map/layer_outputs/pallas_call | solution.py:350
  246.2 2.8 collective-permute-start.16
  249.1 7.6 %collective-permute-done.16 = bf16[144,512]{1,0:T(8,128)(2,1)S(1)} collective-permute-done((bf16[144,512]{1,0:T(8,128)(2,1)S(1)}, bf16[144,512]{1,0:T(8,128)(2,1)S(1)}, u32[]{:S(2)}, u32[]{:S(2)}) %collective-permute-start.16) | collective-permute-done | bytes 147488 | tf_op jit(solution)/shard_map/ppermute | solution.py:818
  257.3 2.8 add_convert_fusion.4
  260.1 1.7 collective-permute-start.19
  261.9 2.6 collective-permute-start.20
  264.7 1.3 copy-done.11
  266.0 6.0 %input_grads.1 = f32[2048,512]{1,0:T(8,128)} custom-call(s32[2]{0:T(128)} %pad_add_fusion.refs_0_, f32[1024,512]{1,0:T(8,128)} %get-tuple-element.116.refs_1_, f32[1024,512]{1,0:T(8,128)} %copy-done.11, bf16[1024,512]{1,0:T(8,128)(2,1)} %get-tuple-element.98.refs_1_.refs_3_, bf16[1024,512]{1,0:T(8,128)(2,1)} %collective-permute-done.11.refs_4_), custom_call_target="tpu_custom_call" | custom-call | flops 1000000 | bytes 8000000 | tf_op jit(solution)/shard_map/input_grads/pallas_call | solution.py:350
  272.4 1.6 collective-permute-start.22
  274.0 1.6 collective-permute-start.24
  275.7 1.4 add_convert_fusion.10
  277.6 3.2 collective-permute-done.24
  282.0 3.8 collective-permute-done.22
  288.4 2.4 collective-permute-done.28
  292.1 1.6 collective-permute-done.26
  293.7 2.0 collective-permute-done.21
  296.4 1.2 collective-permute-start.31
  297.7 8.6 %collective-permute-done.31 = bf16[208,512]{1,0:T(8,128)(2,1)S(1)} collective-permute-done((bf16[208,512]{1,0:T(8,128)(2,1)S(1)}, bf16[208,512]{1,0:T(8,128)(2,1)S(1)}, u32[]{:S(2)}, u32[]{:S(2)}) %collective-permute-start.31) | collective-permute-done | bytes 213024 | tf_op jit(solution)/shard_map/ppermute | solution.py:818
  306.6 1.8 collective-permute-start.30
  308.7 7.3 %collective-permute-done.30 = bf16[2,64,512]{2,1,0:T(8,128)(2,1)S(1)} collective-permute-done((bf16[2,64,512]{2,1,0:T(8,128)(2,1)S(1)}, bf16[2,64,512]{2,1,0:T(8,128)(2,1)S(1)}, u32[]{:S(2)}, u32[]{:S(2)}) %collective-permute-start.30) | collective-permute-done | bytes 131104 | tf_op jit(solution)/shard_map/ppermute | solution.py:834
  316.0 2.1 collective-permute-done.25
  318.2 2.4 collective-permute-start.37
  320.6 2.9 collective-permute-start.29
  323.6 2.9 collective-permute-done.33
  327.5 3.8 collective-permute-done.37
  331.5 2.1 collective-permute-start.34
  333.7 3.2 collective-permute-done.34
  336.9 11.2 %collective-permute-start.40 = (bf16[8,208,512]{2,1,0:T(8,128)(2,1)S(1)}, bf16[8,208,512]{2,1,0:T(8,128)(2,1)S(1)}, u32[]{:S(2)}, u32[]{:S(2)}) collective-permute-start(bf16[8,208,512]{2,1,0:T(8,128)(2,1)S(1)} %pad_maximum_fusion.1.refs_1_.refs_5_), channel_id=1, source_target_pairs={{0,16},{16,0},{1,17},{17,1},{2,18},{18,2},{3,19},{19,3},{4,20},{20... | collective-permute-start | bytes 5111816 | tf_op jit(solution)/shard_map/ppermute | solution.py:810
  348.1 5.3 %collective-permute-done.39.refs_2_.refs_6_ = bf16[8,208,512]{2,1,0:T(8,128)(2,1)S(1)} collective-permute-done((bf16[8,208,512]{2,1,0:T(8,128)(2,1)S(1)}, bf16[8,208,512]{2,1,0:T(8,128)(2,1)S(1)}, u32[]{:S(2)}, u32[]{:S(2)}) %collective-permute-start.39) | collective-permute-done | bytes 1703968 | tf_op jit(solution)/shard_map/ppermute | solution.py:834
  353.4 11.2 %collective-permute-start.41 = (bf16[8,208,512]{2,1,0:T(8,128)(2,1)S(1)}, bf16[8,208,512]{2,1,0:T(8,128)(2,1)}, u32[]{:S(2)}, u32[]{:S(2)}) collective-permute-start(bf16[8,208,512]{2,1,0:T(8,128)(2,1)S(1)} %collective-permute-done.39.refs_2_.refs_6_), channel_id=1, source_target_pairs={{0,16},{16,0},{1,17},{17,1},{2,18},{18,2},{3,19},{19,3},{4,20},{20... | collective-permute-start | bytes 5111816 | tf_op jit(solution)/shard_map/ppermute | solution.py:810
  364.6 2.0 collective-permute-start.42
  366.6 1.4 collective-permute-start.43
  368.0 5.0 %collective-permute-done.36 = bf16[2,64,512]{2,1,0:T(8,128)(2,1)S(1)} collective-permute-done((bf16[2,64,512]{2,1,0:T(8,128)(2,1)S(1)}, bf16[2,64,512]{2,1,0:T(8,128)(2,1)S(1)}, u32[]{:S(2)}, u32[]{:S(2)}) %collective-permute-start.36) | collective-permute-done | bytes 131104 | tf_op jit(solution)/shard_map/ppermute | solution.py:834
  374.8 1.2 copy-done.2
  376.0 6.2 %unpack_ffn.1 = (f32[512,2048]{1,0:T(8,128)}, f32[512,512]{1,0:T(8,128)}, f32[2048,512]{1,0:T(8,128)}) custom-call(s32[2]{0:T(128)} %pad_add_fusion.refs_0_, bf16[8,208,512]{2,1,0:T(8,128)(2,1)} %copy-done, bf16[8,208,512]{2,1,0:T(8,128)(2,1)} %copy-done.1, bf16[8,208,512]{2,1,0:T(8,128)(2,1)} %copy-done.2, ...), custom_call_target="tpu_custom_call" | custom-call | flops 1000000 | bytes 14155776 | tf_op jit(solution)/shard_map/unpack_ffn/pallas_call | solution.py:350
  382.3 1.8 collective-permute-start.44
  385.4 1.3 collective-permute-start.45
  386.6 4.9 %collective-permute-done.44.refs_2_ = bf16[8,64,512]{2,1,0:T(8,128)(2,1)S(1)} collective-permute-done((bf16[8,64,512]{2,1,0:T(8,128)(2,1)S(1)}, bf16[8,64,512]{2,1,0:T(8,128)(2,1)S(1)}, u32[]{:S(2)}, u32[]{:S(2)}) %collective-permute-start.44) | collective-permute-done | bytes 524320 | tf_op jit(solution)/shard_map/ppermute | solution.py:834
  391.6 1.3 collective-permute-start.46
  394.1 1.3 collective-permute-done.46.refs_4_
  396.2 4.1 %unpack_in.1 = f32[512,2048]{1,0:T(8,128)} custom-call(s32[2]{0:T(128)} %pad_add_fusion.refs_0_, bf16[8,64,512]{2,1,0:T(8,128)(2,1)} %copy-done.10, bf16[8,64,512]{2,1,0:T(8,128)(2,1)} %copy-done.21, bf16[8,64,512]{2,1,0:T(8,128)(2,1)} %copy-done.22, bf16[8,64,512]{2,1,0:T(8,128)(2,1)} %copy-done.23, bf16[8,208,512]{2,1,0:T(8,128)(2,1)} %copy-done, ...), custom_call_target="tpu_custom_call" | custom-call | flops 1000000 | bytes 6291456 | tf_op jit(solution)/shard_map/unpack_in/pallas_call | solution.py:350
  (166 shorter events, 23.2 us)
Async XLA Ops:
  0.6 10.3 %collective-permute-start.1 = (bf16[512,2048]{1,0:T(8,128)(2,1)}, bf16[512,2048]{1,0:T(8,128)(2,1)S(1)}, u32[]{:S(2)}, u32[]{:S(2)}) collective-permute-start(bf16[512,2048]{1,0:T(8,128)(2,1)} %bitcast.162), channel_id=1, source_target_pairs={{0,16},{16,0},{1,17},{17,1},{2,18},{18,2},{3,19},{19,3},{4,20},{20... | collective-permute-start | bytes 6291464 | tf_op jit(solution)/shard_map/ppermute | solution.py:810
  1.2 9.8 %collective-permute-start.3 = (bf16[512,2048]{1,0:T(8,128)(2,1)}, bf16[512,2048]{1,0:T(8,128)(2,1)}, u32[]{:S(2)}, u32[]{:S(2)}) collective-permute-start(bf16[512,2048]{1,0:T(8,128)(2,1)} %bitcast.154), channel_id=1, source_target_pairs={{0,16},{16,0},{1,17},{17,1},{2,18},{18,2},{3,19},{19,3},{4,20},{20... | collective-permute-start | bytes 6291464 | tf_op jit(solution)/shard_map/ppermute | solution.py:810
  1.2 10.8 %collective-permute-start.4 = (bf16[2048,512]{1,0:T(8,128)(2,1)}, bf16[2048,512]{1,0:T(8,128)(2,1)}, u32[]{:S(2)}, u32[]{:S(2)}) collective-permute-start(bf16[2048,512]{1,0:T(8,128)(2,1)} %bitcast.158), channel_id=1, source_target_pairs={{0,16},{16,0},{1,17},{17,1},{2,18},{18,2},{3,19},{19,3},{4,20},{20... | collective-permute-start | bytes 6291464 | tf_op jit(solution)/shard_map/ppermute | solution.py:810
  3.3 7.0 %collective-permute-start = (bf16[16,512]{1,0:T(8,128)(2,1)S(1)}, bf16[16,512]{1,0:T(8,128)(2,1)S(1)}, u32[]{:S(2)}, u32[]{:S(2)}) collective-permute-start(bf16[16,512]{1,0:T(8,128)(2,1)S(1)} %concatenate.21), channel_id=1, source_target_pairs={{0,16},{16,0},{1,17},{17,1},{2,18},{18,2},{3,19},{19,3},{4,20},{20... | collective-permute-start | bytes 49160 | tf_op jit(solution)/shard_map/ppermute | solution.py:810
  3.4 7.5 %collective-permute-start.2 = (bf16[512,512]{1,0:T(8,128)(2,1)}, bf16[512,512]{1,0:T(8,128)(2,1)S(1)}, u32[]{:S(2)}, u32[]{:S(2)}) collective-permute-start(bf16[512,512]{1,0:T(8,128)(2,1)} %bitcast.168), channel_id=1, source_target_pairs={{0,16},{16,0},{1,17},{17,1},{2,18},{18,2},{3,19},{19,3},{4,20},{20... | collective-permute-start | bytes 1572872 | tf_op jit(solution)/shard_map/ppermute | solution.py:810
  99.5 32.2 %collective-permute-start.7 = (bf16[16,144,512]{2,1,0:T(8,128)(2,1)}, bf16[16,144,512]{2,1,0:T(8,128)(2,1)S(1)}, u32[]{:S(2)}, u32[]{:S(2)}) collective-permute-start(bf16[16,144,512]{2,1,0:T(8,128)(2,1)} %get-tuple-element.104), channel_id=1, source_target_pairs={{0,16},{16,0},{1,17},{17,1},{2,18},{18,2},{3,19},{19,3},{4,20},{20... | collective-permute-start | bytes 7077896 | tf_op jit(solution)/shard_map/ppermute | solution.py:810
  99.7 32.1 %copy-start.7 = (bf16[16,144,512]{2,1,0:T(8,128)(2,1)S(1)}, bf16[16,144,512]{2,1,0:T(8,128)(2,1)}, u32[]{:S(2)}) copy-start(bf16[16,144,512]{2,1,0:T(8,128)(2,1)} %get-tuple-element.97.refs_11_) | copy-start | bytes 7077892
  133.5 17.1 %collective-permute-start.8 = (bf16[8,144,512]{2,1,0:T(8,128)(2,1)S(1)}, bf16[8,144,512]{2,1,0:T(8,128)(2,1)S(1)}, u32[]{:S(2)}, u32[]{:S(2)}) collective-permute-start(bf16[8,144,512]{2,1,0:T(8,128)(2,1)S(1)} %get-tuple-element.161.refs_3_), channel_id=1, source_target_pairs={{0,1},{1,0},{2,3},{3,2},{4,5},{5,4},{6,7},{7,6},{8,9},{9,8},{10,11... | collective-permute-start | bytes 3538952 | tf_op jit(solution)/shard_map/ppermute | solution.py:834
  136.5 14.2 %copy-start.6 = (bf16[8,144,512]{2,1,0:T(8,128)(2,1)S(1)}, bf16[8,144,512]{2,1,0:T(8,128)(2,1)}, u32[]{:S(2)}) copy-start(bf16[8,144,512]{2,1,0:T(8,128)(2,1)} %get-tuple-element.162.refs_4_) | copy-start | bytes 3538948
  152.0 21.3 %copy-start.19 = (bf16[16,64,512]{2,1,0:T(8,128)(2,1)S(1)}, bf16[16,64,512]{2,1,0:T(8,128)(2,1)}, u32[]{:S(2)}) copy-start(bf16[16,64,512]{2,1,0:T(8,128)(2,1)} %get-tuple-element.124) | copy-start | bytes 3145732
  173.4 12.9 %copy-start.18 = (bf16[16,64,512]{2,1,0:T(8,128)(2,1)S(1)}, bf16[16,64,512]{2,1,0:T(8,128)(2,1)}, u32[]{:S(2)}) copy-start(bf16[16,64,512]{2,1,0:T(8,128)(2,1)} %get-tuple-element.109) | copy-start | bytes 3145732
  173.4 13.0 %copy-start.9 = (bf16[16,144,512]{2,1,0:T(8,128)(2,1)S(1)}, bf16[16,144,512]{2,1,0:T(8,128)(2,1)}, u32[]{:S(2)}) copy-start(bf16[16,144,512]{2,1,0:T(8,128)(2,1)} %get-tuple-element.113) | copy-start | bytes 7077892
  177.2 50.5 %collective-permute-start.13 = (bf16[16,208,512]{2,1,0:T(8,128)(2,1)}, bf16[16,208,512]{2,1,0:T(8,128)(2,1)}, u32[]{:S(2)}, u32[]{:S(2)}) collective-permute-start(bf16[16,208,512]{2,1,0:T(8,128)(2,1)} %pad_maximum_fusion), channel_id=1, source_target_pairs={{0,16},{16,0},{1,17},{17,1},{2,18},{18,2},{3,19},{19,3},{4,20},{20... | collective-permute-start | bytes 10223624 | tf_op jit(solution)/shard_map/ppermute | solution.py:810
  177.2 9.9 %collective-permute-start.9 = (bf16[4,144,512]{2,1,0:T(8,128)(2,1)S(1)}, bf16[4,144,512]{2,1,0:T(8,128)(2,1)S(1)}, u32[]{:S(2)}, u32[]{:S(2)}) collective-permute-start(bf16[4,144,512]{2,1,0:T(8,128)(2,1)S(1)} %copy-done.20), channel_id=1, source_target_pairs={{0,2},{1,3},{2,0},{3,1},{4,6},{5,7},{6,4},{7,5},{8,10},{9,11},{10,... | collective-permute-start | bytes 1769480 | tf_op jit(solution)/shard_map/ppermute | solution.py:834
  179.3 60.3 %collective-permute-start.5 = (f32[1024,512]{1,0:T(8,128)}, f32[1024,512]{1,0:T(8,128)}, u32[]{:S(2)}, u32[]{:S(2)}) collective-permute-start(f32[1024,512]{1,0:T(8,128)} %get-tuple-element.85.refs_2_.refs_1_), channel_id=1, source_target_pairs={{16,0},{17,1},{18,2},{19,3},{20,4},{21,5},{22,6},{23,7},{24,8},{25... | collective-permute-start | bytes 6291464 | tf_op jit(solution)/shard_map/ppermute | solution.py:814
  180.6 56.1 %collective-permute-start.6 = (f32[1024,512]{1,0:T(8,128)}, f32[1024,512]{1,0:T(8,128)}, u32[]{:S(2)}, u32[]{:S(2)}) collective-permute-start(f32[1024,512]{1,0:T(8,128)} %get-tuple-element.86.refs_3_), channel_id=1, source_target_pairs={{0,16},{1,17},{2,18},{3,19},{4,20},{5,21},{6,22},{7,23},{8,24},{9,... | collective-permute-start | bytes 6291464 | tf_op jit(solution)/shard_map/ppermute | solution.py:814
  227.7 8.9 %copy-start.30 = (f32[1,512]{1,0:T(1,128)S(1)}, f32[1,512]{1,0:T(1,128)}, u32[]{:S(2)}) copy-start(f32[1,512]{1,0:T(1,128)} %get-tuple-element.119) | copy-start | bytes 6148
  227.7 8.9 %copy-start.31 = (f32[1,512]{1,0:T(1,128)S(1)}, f32[1,512]{1,0:T(1,128)}, u32[]{:S(2)}) copy-start(f32[1,512]{1,0:T(1,128)} %get-tuple-element.120) | copy-start | bytes 6148
  227.7 8.9 %copy-start.26 = (f32[16,512]{1,0:T(8,128)S(1)}, f32[16,512]{1,0:T(8,128)}, u32[]{:S(2)}) copy-start(f32[16,512]{1,0:T(8,128)} %get-tuple-element.118) | copy-start | bytes 98308
  232.0 25.3 %collective-permute-start.14 = (bf16[8,208,512]{2,1,0:T(8,128)(2,1)}, bf16[8,208,512]{2,1,0:T(8,128)(2,1)}, u32[]{:S(2)}, u32[]{:S(2)}) collective-permute-start(bf16[8,208,512]{2,1,0:T(8,128)(2,1)} %get-tuple-element.159), channel_id=1, source_target_pairs={{0,1},{1,0},{2,3},{3,2},{4,5},{5,4},{6,7},{7,6},{8,9},{9,8},{10,11... | collective-permute-start | bytes 5111816 | tf_op jit(solution)/shard_map/ppermute | solution.py:834
  233.6 31.1 %collective-permute-start.10 = (f32[1024,512]{1,0:T(8,128)}, f32[1024,512]{1,0:T(8,128)S(1)}, u32[]{:S(2)}, u32[]{:S(2)}) collective-permute-start(f32[1024,512]{1,0:T(8,128)} %get-tuple-element.116.refs_1_), channel_id=1, source_target_pairs={{16,0},{17,1},{18,2},{19,3},{20,4},{21,5},{22,6},{23,7},{24,8},{25... | collective-permute-start | bytes 6291464 | tf_op jit(solution)/shard_map/ppermute | solution.py:814
  234.9 11.3 %collective-permute-start.15 = (bf16[2,144,512]{2,1,0:T(8,128)(2,1)}, bf16[2,144,512]{2,1,0:T(8,128)(2,1)S(1)}, u32[]{:S(2)}, u32[]{:S(2)}) collective-permute-start(bf16[2,144,512]{2,1,0:T(8,128)(2,1)} %get-tuple-element.172.refs_12_), channel_id=1, source_target_pairs={{0,4},{1,5},{2,6},{3,7},{4,0},{5,1},{6,2},{7,3},{8,12},{9,13},{10,... | collective-permute-start | bytes 884744 | tf_op jit(solution)/shard_map/ppermute | solution.py:834
  236.7 9.5 %copy-start.16 = (bf16[2,1,144,512]{3,2,0,1:T(8,128)(2,1)S(1)}, bf16[2,1,144,512]{3,2,0,1:T(8,128)(2,1)}, u32[]{:S(2)}) copy-start(bf16[2,1,144,512]{3,2,0,1:T(8,128)(2,1)} %get-tuple-element.171) | copy-start | bytes 884740
  236.7 12.4 %copy-start.28 = (f32[16,512]{1,0:T(8,128)S(1)}, f32[16,512]{1,0:T(8,128)}, u32[]{:S(2)}) copy-start(f32[16,512]{1,0:T(8,128)} %get-tuple-element.114) | copy-start | bytes 98308
  236.7 12.3 %copy-start.29 = (f32[16,512]{1,0:T(8,128)S(1)}, f32[16,512]{1,0:T(8,128)}, u32[]{:S(2)}) copy-start(f32[16,512]{1,0:T(8,128)} %get-tuple-element.117) | copy-start | bytes 98308
  236.7 27.9 %collective-permute-start.11 = (bf16[1024,512]{1,0:T(8,128)(2,1)}, bf16[1024,512]{1,0:T(8,128)(2,1)}, u32[]{:S(2)}, u32[]{:S(2)}) collective-permute-start(bf16[1024,512]{1,0:T(8,128)(2,1)} %get-tuple-element.98.refs_1_.refs_3_), channel_id=1, source_target_pairs={{0,16},{1,17},{2,18},{3,19},{4,20},{5,21},{6,22},{7,23},{8,24},{9,... | collective-permute-start | bytes 3145736 | tf_op jit(solution)/shard_map/ppermute | solution.py:814
  246.2 25.9 %collective-permute-start.18 = (bf16[16,64,512]{2,1,0:T(8,128)(2,1)}, bf16[16,64,512]{2,1,0:T(8,128)(2,1)S(1)}, u32[]{:S(2)}, u32[]{:S(2)}) collective-permute-start(bf16[16,64,512]{2,1,0:T(8,128)(2,1)} %get-tuple-element.131), channel_id=1, source_target_pairs={{0,16},{16,0},{1,17},{17,1},{2,18},{18,2},{3,19},{19,3},{4,20},{20... | collective-permute-start | bytes 3145736 | tf_op jit(solution)/shard_map/ppermute | solution.py:810
  246.2 11.1 %copy-start.24 = (bf16[2,144,512]{2,1,0:T(8,128)(2,1)}, bf16[2,144,512]{2,1,0:T(8,128)(2,1)S(1)}, u32[]{:S(2)}) copy-start(bf16[2,144,512]{2,1,0:T(8,128)(2,1)S(1)} %collective-permute-done.15) | copy-start | bytes 884740
  246.2 10.5 %collective-permute-start.16 = (bf16[144,512]{1,0:T(8,128)(2,1)S(1)}, bf16[144,512]{1,0:T(8,128)(2,1)S(1)}, u32[]{:S(2)}, u32[]{:S(2)}) collective-permute-start(bf16[144,512]{1,0:T(8,128)(2,1)S(1)} %fusion.10), channel_id=1, source_target_pairs={{0,8},{4,12},{8,0},{12,4},{1,9},{5,13},{9,1},{13,5},{2,10},{6,14},... | collective-permute-start | bytes 442376 | tf_op jit(solution)/shard_map/ppermute | solution.py:818
  260.1 15.5 %collective-permute-start.19 = (bf16[4,208,512]{2,1,0:T(8,128)(2,1)}, bf16[4,208,512]{2,1,0:T(8,128)(2,1)}, u32[]{:S(2)}, u32[]{:S(2)}) collective-permute-start(bf16[4,208,512]{2,1,0:T(8,128)(2,1)} %get-tuple-element.164), channel_id=1, source_target_pairs={{0,2},{1,3},{2,0},{3,1},{4,6},{5,7},{6,4},{7,5},{8,10},{9,11},{10,... | collective-permute-start | bytes 2555912 | tf_op jit(solution)/shard_map/ppermute | solution.py:834
  261.9 10.2 %collective-permute-start.20 = (bf16[144,512]{1,0:T(8,128)(2,1)S(1)}, bf16[144,512]{1,0:T(8,128)(2,1)S(1)}, u32[]{:S(2)}, u32[]{:S(2)}) collective-permute-start(bf16[144,512]{1,0:T(8,128)(2,1)S(1)} %fusion.5), channel_id=1, source_target_pairs={{0,8},{4,12},{8,0},{12,4},{1,9},{5,13},{9,1},{13,5},{2,10},{6,14},... | collective-permute-start | bytes 442376 | tf_op jit(solution)/shard_map/ppermute | solution.py:818
  264.6 11.0 %collective-permute-start.12 = (f32[24,512]{1,0:T(8,128)S(1)}, f32[24,512]{1,0:T(8,128)S(1)}, u32[]{:S(2)}, u32[]{:S(2)}) collective-permute-start(f32[24,512]{1,0:T(8,128)S(1)} %maximum_maximum_fusion), channel_id=1, source_target_pairs={{0,16},{16,0},{1,17},{17,1},{2,18},{18,2},{3,19},{19,3},{4,20},{20... | collective-permute-start | bytes 147464 | tf_op jit(solution)/shard_map/ppermute | solution.py:818
  272.4 13.4 %collective-permute-start.22 = (bf16[8,64,512]{2,1,0:T(8,128)(2,1)S(1)}, bf16[8,64,512]{2,1,0:T(8,128)(2,1)S(1)}, u32[]{:S(2)}, u32[]{:S(2)}) collective-permute-start(bf16[8,64,512]{2,1,0:T(8,128)(2,1)S(1)} %get-tuple-element.168), channel_id=1, source_target_pairs={{0,1},{1,0},{2,3},{3,2},{4,5},{5,4},{6,7},{7,6},{8,9},{9,8},{10,11... | collective-permute-start | bytes 1572872 | tf_op jit(solution)/shard_map/ppermute | solution.py:834
  274.0 6.8 %collective-permute-start.24 = (bf16[2,144,512]{2,1,0:T(8,128)(2,1)S(1)}, bf16[2,144,512]{2,1,0:T(8,128)(2,1)S(1)}, u32[]{:S(2)}, u32[]{:S(2)}) collective-permute-start(bf16[2,144,512]{2,1,0:T(8,128)(2,1)S(1)} %get-tuple-element.182), channel_id=1, source_target_pairs={{0,4},{1,5},{2,6},{3,7},{4,0},{5,1},{6,2},{7,3},{8,12},{9,13},{10,... | collective-permute-start | bytes 884744 | tf_op jit(solution)/shard_map/ppermute | solution.py:834
  277.1 10.9 %collective-permute-start.23 = (bf16[2,208,512]{2,1,0:T(8,128)(2,1)S(1)}, bf16[2,208,512]{2,1,0:T(8,128)(2,1)S(1)}, u32[]{:S(2)}, u32[]{:S(2)}) collective-permute-start(bf16[2,208,512]{2,1,0:T(8,128)(2,1)S(1)} %get-tuple-element.170), channel_id=1, source_target_pairs={{0,4},{1,5},{2,6},{3,7},{4,0},{5,1},{6,2},{7,3},{8,12},{9,13},{10,... | collective-permute-start | bytes 1277960 | tf_op jit(solution)/shard_map/ppermute | solution.py:834
  280.9 9.9 %collective-permute-start.28 = (bf16[4,144,512]{2,1,0:T(8,128)(2,1)S(1)}, bf16[4,144,512]{2,1,0:T(8,128)(2,1)S(1)}, u32[]{:S(2)}, u32[]{:S(2)}) collective-permute-start(bf16[4,144,512]{2,1,0:T(8,128)(2,1)S(1)} %bitcast.131), channel_id=1, source_target_pairs={{0,2},{1,3},{2,0},{3,1},{4,6},{5,7},{6,4},{7,5},{8,10},{9,11},{10,... | collective-permute-start | bytes 1769480 | tf_op jit(solution)/shard_map/ppermute | solution.py:834
  281.5 5.4 %collective-permute-start.17 = (f32[24,512]{1,0:T(8,128)S(1)}, f32[24,512]{1,0:T(8,128)S(1)}, u32[]{:S(2)}, u32[]{:S(2)}) collective-permute-start(f32[24,512]{1,0:T(8,128)S(1)} %add.142), channel_id=1, source_target_pairs={{0,1},{1,0},{2,3},{3,2},{4,5},{5,4},{6,7},{7,6},{8,9},{9,8},{10,11... | collective-permute-start | bytes 147464 | tf_op jit(solution)/shard_map/ppermute | solution.py:818
  287.1 6.6 %collective-permute-start.26 = (bf16[4,64,512]{2,1,0:T(8,128)(2,1)S(1)}, bf16[4,64,512]{2,1,0:T(8,128)(2,1)S(1)}, u32[]{:S(2)}, u32[]{:S(2)}) collective-permute-start(bf16[4,64,512]{2,1,0:T(8,128)(2,1)S(1)} %get-tuple-element.174), channel_id=1, source_target_pairs={{0,2},{1,3},{2,0},{3,1},{4,6},{5,7},{6,4},{7,5},{8,10},{9,11},{10,... | collective-permute-start | bytes 786440 | tf_op jit(solution)/shard_map/ppermute | solution.py:834
  288.0 8.3 %collective-permute-start.27 = (bf16[208,512]{1,0:T(8,128)(2,1)S(1)}, bf16[208,512]{1,0:T(8,128)(2,1)S(1)}, u32[]{:S(2)}, u32[]{:S(2)}) collective-permute-start(bf16[208,512]{1,0:T(8,128)(2,1)S(1)} %get-tuple-element.176), channel_id=1, source_target_pairs={{0,8},{4,12},{8,0},{12,4},{1,9},{5,13},{9,1},{13,5},{2,10},{6,14},... | collective-permute-start | bytes 638984 | tf_op jit(solution)/shard_map/ppermute | solution.py:818
  291.0 73.6 %copy-start.5 = (bf16[8,144,512]{2,1,0:T(8,128)(2,1)}, bf16[8,144,512]{2,1,0:T(8,128)(2,1)S(1)}, u32[]{:S(2)}) copy-start(bf16[8,144,512]{2,1,0:T(8,128)(2,1)S(1)} %pad_maximum_fusion.2.refs_5_) | copy-start | bytes 3538948
  291.0 27.1 %collective-permute-start.32 = (bf16[8,144,512]{2,1,0:T(8,128)(2,1)S(1)}, bf16[8,144,512]{2,1,0:T(8,128)(2,1)S(1)}, u32[]{:S(2)}, u32[]{:S(2)}) collective-permute-start(bf16[8,144,512]{2,1,0:T(8,128)(2,1)S(1)} %pad_maximum_fusion.2.refs_5_), channel_id=1, source_target_pairs={{0,1},{1,0},{2,3},{3,2},{4,5},{5,4},{6,7},{7,6},{8,9},{9,8},{10,11... | collective-permute-start | bytes 3538952 | tf_op jit(solution)/shard_map/ppermute | solution.py:834
  291.6 4.1 %collective-permute-start.21 = (f32[24,512]{1,0:T(8,128)S(1)}, f32[24,512]{1,0:T(8,128)S(1)}, u32[]{:S(2)}, u32[]{:S(2)}) collective-permute-start(f32[24,512]{1,0:T(8,128)S(1)} %add.147), channel_id=1, source_target_pairs={{0,2},{1,3},{2,0},{3,1},{4,6},{5,7},{6,4},{7,5},{8,10},{9,11},{10,... | collective-permute-start | bytes 147464 | tf_op jit(solution)/shard_map/ppermute | solution.py:818
  296.4 9.9 %collective-permute-start.31 = (bf16[208,512]{1,0:T(8,128)(2,1)S(1)}, bf16[208,512]{1,0:T(8,128)(2,1)S(1)}, u32[]{:S(2)}, u32[]{:S(2)}) collective-permute-start(bf16[208,512]{1,0:T(8,128)(2,1)S(1)} %add_convert_fusion.16), channel_id=1, source_target_pairs={{0,8},{4,12},{8,0},{12,4},{1,9},{5,13},{9,1},{13,5},{2,10},{6,14},... | collective-permute-start | bytes 638984 | tf_op jit(solution)/shard_map/ppermute | solution.py:818
  306.4 11.8 %collective-permute-start.35 = (bf16[2,208,512]{2,1,0:T(8,128)(2,1)S(1)}, bf16[2,208,512]{2,1,0:T(8,128)(2,1)S(1)}, u32[]{:S(2)}, u32[]{:S(2)}) collective-permute-start(bf16[2,208,512]{2,1,0:T(8,128)(2,1)S(1)} %get-tuple-element.180), channel_id=1, source_target_pairs={{0,4},{1,5},{2,6},{3,7},{4,0},{5,1},{6,2},{7,3},{8,12},{9,13},{10,... | collective-permute-start | bytes 1277960 | tf_op jit(solution)/shard_map/ppermute | solution.py:834
  306.6 9.3 %collective-permute-start.30 = (bf16[2,64,512]{2,1,0:T(8,128)(2,1)S(1)}, bf16[2,64,512]{2,1,0:T(8,128)(2,1)S(1)}, u32[]{:S(2)}, u32[]{:S(2)}) collective-permute-start(bf16[2,64,512]{2,1,0:T(8,128)(2,1)S(1)} %get-tuple-element.178), channel_id=1, source_target_pairs={{0,4},{1,5},{2,6},{3,7},{4,0},{5,1},{6,2},{7,3},{8,12},{9,13},{10,... | collective-permute-start | bytes 393224 | tf_op jit(solution)/shard_map/ppermute | solution.py:834
  308.5 9.6 %collective-permute-start.25 = (f32[24,512]{1,0:T(8,128)S(1)}, f32[24,512]{1,0:T(8,128)S(1)}, u32[]{:S(2)}, u32[]{:S(2)}) collective-permute-start(f32[24,512]{1,0:T(8,128)S(1)} %add.152), channel_id=1, source_target_pairs={{0,4},{4,0},{8,12},{12,8},{1,5},{5,1},{9,13},{13,9},{2,6},{6,2},{1... | collective-permute-start | bytes 147464 | tf_op jit(solution)/shard_map/ppermute | solution.py:818
  318.1 48.4 %copy-start.12 = (bf16[8,144,512]{2,1,0:T(8,128)(2,1)}, bf16[8,144,512]{2,1,0:T(8,128)(2,1)S(1)}, u32[]{:S(2)}) copy-start(bf16[8,144,512]{2,1,0:T(8,128)(2,1)S(1)} %collective-permute-done.32.refs_6_) | copy-start | bytes 3538948
  318.2 13.1 %collective-permute-start.37 = (bf16[4,208,512]{2,1,0:T(8,128)(2,1)S(1)}, bf16[4,208,512]{2,1,0:T(8,128)(2,1)S(1)}, u32[]{:S(2)}, u32[]{:S(2)}) collective-permute-start(bf16[4,208,512]{2,1,0:T(8,128)(2,1)S(1)} %bitcast.128), channel_id=1, source_target_pairs={{0,2},{1,3},{2,0},{3,1},{4,6},{5,7},{6,4},{7,5},{8,10},{9,11},{10,... | collective-permute-start | bytes 2555912 | tf_op jit(solution)/shard_map/ppermute | solution.py:834
  320.6 5.8 %collective-permute-start.33 = (bf16[64,512]{1,0:T(8,128)(2,1)S(1)}, bf16[64,512]{1,0:T(8,128)(2,1)S(1)}, u32[]{:S(2)}, u32[]{:S(2)}) collective-permute-start(bf16[64,512]{1,0:T(8,128)(2,1)S(1)} %get-tuple-element.184), channel_id=1, source_target_pairs={{0,8},{4,12},{8,0},{12,4},{1,9},{5,13},{9,1},{13,5},{2,10},{6,14},... | collective-permute-start | bytes 196616 | tf_op jit(solution)/shard_map/ppermute | solution.py:818
  320.6 6.8 %collective-permute-start.29 = (f32[24,512]{1,0:T(8,128)S(1)}, f32[24,512]{1,0:T(8,128)S(1)}, u32[]{:S(2)}, u32[]{:S(2)}) collective-permute-start(f32[24,512]{1,0:T(8,128)S(1)} %add.156), channel_id=1, source_target_pairs={{0,8},{4,12},{8,0},{12,4},{1,9},{5,13},{9,1},{13,5},{2,10},{6,14},... | collective-permute-start | bytes 147464 | tf_op jit(solution)/shard_map/ppermute | solution.py:818
  331.5 43.3 %copy-start = (bf16[8,208,512]{2,1,0:T(8,128)(2,1)}, bf16[8,208,512]{2,1,0:T(8,128)(2,1)S(1)}, u32[]{:S(2)}) copy-start(bf16[8,208,512]{2,1,0:T(8,128)(2,1)S(1)} %pad_maximum_fusion.1.refs_1_.refs_5_) | copy-start | bytes 5111812
  331.5 21.9 %collective-permute-start.39 = (bf16[8,208,512]{2,1,0:T(8,128)(2,1)S(1)}, bf16[8,208,512]{2,1,0:T(8,128)(2,1)S(1)}, u32[]{:S(2)}, u32[]{:S(2)}) collective-permute-start(bf16[8,208,512]{2,1,0:T(8,128)(2,1)S(1)} %pad_maximum_fusion.1.refs_1_.refs_5_), channel_id=1, source_target_pairs={{0,1},{1,0},{2,3},{3,2},{4,5},{5,4},{6,7},{7,6},{8,9},{9,8},{10,11... | collective-permute-start | bytes 5111816 | tf_op jit(solution)/shard_map/ppermute | solution.py:834
  331.5 5.3 %collective-permute-start.34 = (bf16[64,512]{1,0:T(8,128)(2,1)S(1)}, bf16[64,512]{1,0:T(8,128)(2,1)S(1)}, u32[]{:S(2)}, u32[]{:S(2)}) collective-permute-start(bf16[64,512]{1,0:T(8,128)(2,1)S(1)} %add_convert_fusion.19), channel_id=1, source_target_pairs={{0,8},{4,12},{8,0},{12,4},{1,9},{5,13},{9,1},{13,5},{2,10},{6,14},... | collective-permute-start | bytes 196616 | tf_op jit(solution)/shard_map/ppermute | solution.py:818
  336.9 36.5 %collective-permute-start.40 = (bf16[8,208,512]{2,1,0:T(8,128)(2,1)S(1)}, bf16[8,208,512]{2,1,0:T(8,128)(2,1)S(1)}, u32[]{:S(2)}, u32[]{:S(2)}) collective-permute-start(bf16[8,208,512]{2,1,0:T(8,128)(2,1)S(1)} %pad_maximum_fusion.1.refs_1_.refs_5_), channel_id=1, source_target_pairs={{0,16},{16,0},{1,17},{17,1},{2,18},{18,2},{3,19},{19,3},{4,20},{20... | collective-permute-start | bytes 5111816 | tf_op jit(solution)/shard_map/ppermute | solution.py:810
  353.3 21.5 %copy-start.1 = (bf16[8,208,512]{2,1,0:T(8,128)(2,1)}, bf16[8,208,512]{2,1,0:T(8,128)(2,1)S(1)}, u32[]{:S(2)}) copy-start(bf16[8,208,512]{2,1,0:T(8,128)(2,1)S(1)} %collective-permute-done.39.refs_2_.refs_6_) | copy-start | bytes 5111812
  353.4 21.4 %collective-permute-start.41 = (bf16[8,208,512]{2,1,0:T(8,128)(2,1)S(1)}, bf16[8,208,512]{2,1,0:T(8,128)(2,1)}, u32[]{:S(2)}, u32[]{:S(2)}) collective-permute-start(bf16[8,208,512]{2,1,0:T(8,128)(2,1)S(1)} %collective-permute-done.39.refs_2_.refs_6_), channel_id=1, source_target_pairs={{0,16},{16,0},{1,17},{17,1},{2,18},{18,2},{3,19},{19,3},{4,20},{20... | collective-permute-start | bytes 5111816 | tf_op jit(solution)/shard_map/ppermute | solution.py:810
  364.6 8.8 %collective-permute-start.42 = (bf16[8,144,512]{2,1,0:T(8,128)(2,1)S(1)}, bf16[8,144,512]{2,1,0:T(8,128)(2,1)S(1)}, u32[]{:S(2)}, u32[]{:S(2)}) collective-permute-start(bf16[8,144,512]{2,1,0:T(8,128)(2,1)S(1)} %pad_maximum_fusion.2.refs_5_), channel_id=1, source_target_pairs={{0,16},{1,17},{2,18},{3,19},{4,20},{5,21},{6,22},{7,23},{8,24},{9,... | collective-permute-start | bytes 3538952 | tf_op jit(solution)/shard_map/ppermute | solution.py:814
  366.6 6.8 %collective-permute-start.43 = (bf16[8,144,512]{2,1,0:T(8,128)(2,1)S(1)}, bf16[8,144,512]{2,1,0:T(8,128)(2,1)S(1)}, u32[]{:S(2)}, u32[]{:S(2)}) collective-permute-start(bf16[8,144,512]{2,1,0:T(8,128)(2,1)S(1)} %collective-permute-done.32.refs_6_), channel_id=1, source_target_pairs={{0,16},{1,17},{2,18},{3,19},{4,20},{5,21},{6,22},{7,23},{8,24},{9,... | collective-permute-start | bytes 3538952 | tf_op jit(solution)/shard_map/ppermute | solution.py:814
  367.9 5.0 %collective-permute-start.36 = (bf16[2,64,512]{2,1,0:T(8,128)(2,1)S(1)}, bf16[2,64,512]{2,1,0:T(8,128)(2,1)S(1)}, u32[]{:S(2)}, u32[]{:S(2)}) collective-permute-start(bf16[2,64,512]{2,1,0:T(8,128)(2,1)S(1)} %get-tuple-element.186), channel_id=1, source_target_pairs={{0,4},{1,5},{2,6},{3,7},{4,0},{5,1},{6,2},{7,3},{8,12},{9,13},{10,... | collective-permute-start | bytes 393224 | tf_op jit(solution)/shard_map/ppermute | solution.py:834
  373.0 9.3 %collective-permute-start.38 = (bf16[4,64,512]{2,1,0:T(8,128)(2,1)S(1)}, bf16[4,64,512]{2,1,0:T(8,128)(2,1)S(1)}, u32[]{:S(2)}, u32[]{:S(2)}) collective-permute-start(bf16[4,64,512]{2,1,0:T(8,128)(2,1)S(1)} %bitcast.136), channel_id=1, source_target_pairs={{0,2},{1,3},{2,0},{3,1},{4,6},{5,7},{6,4},{7,5},{8,10},{9,11},{10,... | collective-permute-start | bytes 786440 | tf_op jit(solution)/shard_map/ppermute | solution.py:834
  382.3 13.1 %copy-start.10 = (bf16[8,64,512]{2,1,0:T(8,128)(2,1)}, bf16[8,64,512]{2,1,0:T(8,128)(2,1)S(1)}, u32[]{:S(2)}) copy-start(bf16[8,64,512]{2,1,0:T(8,128)(2,1)S(1)} %pad_maximum_fusion.5.refs_1_) | copy-start | bytes 1572868
  382.3 9.2 %collective-permute-start.44 = (bf16[8,64,512]{2,1,0:T(8,128)(2,1)S(1)}, bf16[8,64,512]{2,1,0:T(8,128)(2,1)S(1)}, u32[]{:S(2)}, u32[]{:S(2)}) collective-permute-start(bf16[8,64,512]{2,1,0:T(8,128)(2,1)S(1)} %pad_maximum_fusion.5.refs_1_), channel_id=1, source_target_pairs={{0,1},{1,0},{2,3},{3,2},{4,5},{5,4},{6,7},{7,6},{8,9},{9,8},{10,11... | collective-permute-start | bytes 1572872 | tf_op jit(solution)/shard_map/ppermute | solution.py:834
  385.4 8.8 %collective-permute-start.45 = (bf16[8,64,512]{2,1,0:T(8,128)(2,1)S(1)}, bf16[8,64,512]{2,1,0:T(8,128)(2,1)S(1)}, u32[]{:S(2)}, u32[]{:S(2)}) collective-permute-start(bf16[8,64,512]{2,1,0:T(8,128)(2,1)S(1)} %pad_maximum_fusion.5.refs_1_), channel_id=1, source_target_pairs={{16,0},{17,1},{18,2},{19,3},{20,4},{21,5},{22,6},{23,7},{24,8},{25... | collective-permute-start | bytes 1572872 | tf_op jit(solution)/shard_map/ppermute | solution.py:814
  391.6 3.8 collective-permute-start.46
  (17 other events, 51.2 us)
